TPU v7x, 256 devices: a whole 4x4x8 slice. The times are simulated.
256 devices in a mesh: hid: 64 (over x, y_lo, z), mod: 4 (over y_hi, core).
Axes of the slice: x: 4, y: 4 (y_hi: 2, y_lo: 2; y = y_hi * 2 + y_lo), z: 8, core: 2. Of those that a mesh axis runs over, the one named last changes fastest.
Arguments:
- tokens: bfloat16 [1024, 8192], P('hid', 'mod'), may hold values from -6 to 6
- grad_output: bfloat16 [1024, 8192], P('hid', 'mod'), may hold values from -6 to 6
- gate_weight: bfloat16 [8192, 28672], P('mod', 'hid'), may hold values from -0.0625 to 0.0625
- up_weight: bfloat16 [8192, 28672], P('mod', 'hid'), may hold values from -0.0625 to 0.0625
- down_weight: bfloat16 [28672, 8192], P('hid', 'mod'), may hold values from -0.03125 to 0.03125
Outputs:
- grad_tokens: bfloat16 [1024, 8192], P('hid', 'mod')
- grad_gate: bfloat16 [8192, 28672], P('mod', 'hid')
- grad_up: bfloat16 [8192, 28672], P('mod', 'hid')
- grad_down: bfloat16 [28672, 8192], P('hid', 'mod')
All inputs are finite; a program needn't handle non-finite values.
Results may differ from a plain program's by a relative error of at most 0.0049.
Values may be sent and summed in bfloat16 or wider, within the bound.
A program may use at most 128 MiB of HBM per device.

v0:
```python
import jax
import jax.numpy as jnp
from jax import lax
from jax.sharding import PartitionSpec as P


def swiglu_back(gate, up, grad_hidden):
    sigmoid_gate = jax.nn.sigmoid(gate)
    active = gate * sigmoid_gate
    hidden = (active * up).astype(jnp.bfloat16)
    up_back = (grad_hidden * active).astype(jnp.bfloat16)
    slope = sigmoid_gate * (1.0 + gate * (1.0 - sigmoid_gate))
    gate_back = (grad_hidden * up * slope).astype(jnp.bfloat16)
    return (hidden, gate_back, up_back)


def shards(tokens, grad_output, gate_weight, up_weight, down_weight):
    inputs, cotangent = (
        lax.all_gather(tokens, "hid", axis=0, tiled=True),
        lax.all_gather(grad_output, "hid", axis=0, tiled=True),
    )
    contract_cols = (((1,), (1,)), ((), ()))
    contract_rows = (((0,), (0,)), ((), ()))
    part_gate = jnp.dot(inputs, gate_weight, preferred_element_type=jnp.float32)
    part_up = jnp.dot(inputs, up_weight, preferred_element_type=jnp.float32)
    part_hidden = lax.dot_general(
        cotangent, down_weight, contract_cols, preferred_element_type=jnp.float32
    )
    gate, up, grad_hidden = lax.psum((part_gate, part_up, part_hidden), "mod")
    hidden, gate_back, up_back = swiglu_back(gate, up, grad_hidden)
    grad_down = lax.dot_general(
        hidden, cotangent, contract_rows, preferred_element_type=jnp.float32
    ).astype(jnp.bfloat16)
    grad_gate = lax.dot_general(
        inputs, gate_back, contract_rows, preferred_element_type=jnp.float32
    ).astype(jnp.bfloat16)
    grad_up = lax.dot_general(
        inputs, up_back, contract_rows, preferred_element_type=jnp.float32
    ).astype(jnp.bfloat16)
    total = lax.dot_general(
        gate_back, gate_weight, contract_cols, preferred_element_type=jnp.float32
    )
    summed = lax.psum_scatter(
        total
        + lax.dot_general(up_back, up_weight, contract_cols, preferred_element_type=jnp.float32),
        "hid",
        scatter_dimension=0,
        tiled=True,
    )
    grad_tokens = summed.astype(jnp.bfloat16)
    return (grad_tokens, grad_gate, grad_up, grad_down)


def solution(mesh):
    placed = (P("hid", "mod"), P("hid", "mod"), P("mod", "hid"), P("mod", "hid"), P("hid", "mod"))
    return jax.shard_map(
        shards,
        mesh=mesh,
        in_specs=placed,
        out_specs=(P("hid", "mod"), P("mod", "hid"), P("mod", "hid"), P("hid", "mod")),
        check_vma=False,
    )
```

profile of v0, /device:TPU:16, one launch (start us, length us, event | category | flops | bytes accessed | tf_op | source)
XLA Modules:
  0.0 1094.7 jit_solution(14310833977302647176)
XLA Ops:
  7.2 0.0 copy-start
  7.2 0.0 all-gather.5.cloned.1.call-start
  7.2 0.7 all-gather.5.cloned.1.call-update
  7.9 0.0 all-gather.3.cloned.1.call-start
  8.0 0.7 all-gather.3.cloned.1.call-update
  8.7 0.0 all-reduce.3.cloned.1.call-start
  8.7 307.6 %all-gather.5.cloned.1.call-done = bf16[1024,2048]{1,0:T(8,128)(2,1)} async-done(((bf16[16,2048]{1,0:T(8,128)(2,1)}), bf16[1024,2048]{1,0:T(8,128)(2,1)}) %all-gather.5.cloned.1.call-update) | async-done | bytes 4194320 | tf_op jit(solution)/shard_map/all_gather | solution.py:19
  316.3 0.0 copy-done
  316.3 0.0 copy-start.1
  316.3 0.0 copy-start.7
  316.3 5.7 fusion.7
  322.0 0.0 copy-done.1
  322.0 0.0 copy-done.7
  322.0 3.3 fusion.6
  325.3 293.9 %all-gather.3.cloned.1.call-done = bf16[1024,2048]{1,0:T(8,128)(2,1)} async-done(((bf16[16,2048]{1,0:T(8,128)(2,1)}), bf16[1024,2048]{1,0:T(8,128)(2,1)}) %all-gather.3.cloned.1.call-update) | async-done | bytes 4194320 | tf_op jit(solution)/shard_map/all_gather | solution.py:20
  619.3 6.1 fusion.5
  625.4 0.0 all-reduce.3.cloned.1.call-update
  625.4 0.2 reduce-scatter.2.cloned.1.call-start
  625.6 113.8 %all-reduce.3.cloned.1.call-done = (f32[1024,448]{0,1:T(8,128)}, f32[1024,448]{0,1:T(8,128)}, f32[1024,448]{0,1:T(8,128)}) async-done(((f32[1024,448]{0,1:T(8,128)}, f32[1024,448]{0,1:T(8,128)}, f32[1024,448]{0,1:T(8,128)}), (f32[1024,448]{0,1:T(8,128)}, f32[1024,448]{0,1:T(8,128)}, f32[1024,448]{0,1:T(8,128)})) %all-reduce.3.cloned.1.call-update) | async-done | bytes 5505040 | tf_op jit(solution)/shard_map/psum | solution.py:29
  739.4 3.7 multiply_convert_fusion.1
  743.2 0.0 copy-start.5
  743.2 0.0 copy-start.2
  743.2 2.4 fusion.8
  745.6 0.0 copy-done.5
  745.6 0.0 copy-done.2
  745.6 5.9 convolution_add_fusion
  751.5 0.0 reduce-scatter.2.cloned.1.call-update
  751.5 0.0 copy-start.6
  751.5 0.0 copy-start.8
  751.6 5.6 fusion.1
  757.2 0.0 copy-done.6
  757.2 0.0 copy-done.8
  757.2 0.0 copy-start.3
  757.2 0.0 copy-start.4
  757.2 0.0 copy-start.9
  757.2 3.3 fusion
  760.5 0.0 copy-done.3
  760.5 0.0 copy-done.4
  760.5 0.4 copy-done.9
  760.9 3.4 convolution_convert_fusion
  764.3 322.4 %reduce-scatter.2.cloned.1.call-done = f32[16,2048]{1,0:T(8,128)} async-done(((f32[1024,2048]{1,0:T(8,128)}), f32[16,2048]{1,0:T(8,128)}) %reduce-scatter.2.cloned.1.call-update) | async-done | bytes 131088 | tf_op jit(solution)/shard_map/reduce_scatter | solution.py:43
  1086.7 1.5 convert_element_type.29
Async XLA Ops:
  7.2 309.2 %copy-start = (bf16[2048,448]{0,1:T(8,128)(2,1)S(1)}, bf16[2048,448]{0,1:T(8,128)(2,1)}, u32[]{:S(2)}) copy-start(bf16[2048,448]{0,1:T(8,128)(2,1)} %param.7) | copy-start | bytes 5505028
  7.2 309.2 %all-gather.5.cloned.1.call-start = ((), (), s32[]{:S(2)}) async-start(), calls=%async_computation.2 | async-start | bytes 4259840 | tf_op jit(solution)/shard_map/all_gather | solution.py:19
  7.9 611.3 %all-gather.3.cloned.1.call-start = ((), (), s32[]{:S(2)}) async-start(), calls=%async_computation.1 | async-start | bytes 4259840 | tf_op jit(solution)/shard_map/all_gather | solution.py:20
  8.7 730.8 %all-reduce.3.cloned.1.call-start = ((), (), s32[]{:S(2)}) async-start(), calls=%async_computation.4 | async-start | bytes 11010048 | tf_op jit(solution)/shard_map/psum | solution.py:29
  316.3 5.7 copy-start.1
  316.3 5.7 copy-start.7
  625.4 461.3 %reduce-scatter.2.cloned.1.call-start = ((), (), s32[]{:S(2)}) async-start(), calls=%async_computation.3 | async-start | bytes 8519680 | tf_op jit(solution)/shard_map/reduce_scatter | solution.py:43
  743.2 2.4 copy-start.5
  743.2 2.4 copy-start.2
  751.5 5.7 copy-start.6
  751.5 5.7 copy-start.8
  757.2 3.4 copy-start.3
  757.2 3.4 copy-start.4
  757.2 3.7 copy-start.9
Sparse Core Ops, SparseCore 0:
  9.8 306.4 all-gather.4
  318.1 301.0 all-gather.2
  625.5 113.8 all-reduce.2
  751.6 334.9 reduce-scatter.1
where the time goes:
time: 1090 us
  waiting for transfers between devices  1040 us (95%)
  matrix products  35.7 us (3%)
  between operations  13.8 us (1%)
    reduce_scatter x1, waiting for transfers between devices, shards(): lax.psum_scatter(total + lax.dot_general(up_back, up_weight, contract_col...  322 us
    all_gather x1, waiting for transfers between devices, shards(): lax.all_gather(tokens, 'hid', axis=0, tiled=True)  308 us
    all_gather x1, waiting for transfers between devices, shards(): lax.all_gather(grad_output, 'hid', axis=0, tiled=True)  294 us
    psum x1, waiting for transfers between devices, shards(): gate, up, grad_hidden = lax.psum((part_gate, part_up, part_hidden), 'mod')  114 us
  transfers between devices with their start and end apart: 4, of which 4 were waited for; matrix products, arithmetic and copies ran while one was open for 2% of the time, Pallas kernels for 0%

commit v1 on v0

v1 whole, which is shorter than its diff:
```python
import functools

import jax
import jax.numpy as jnp
from jax import lax
from jax.experimental import pallas as pl
from jax.experimental.pallas import tpu as pltpu
from jax.sharding import PartitionSpec as P

MESH = pl.DeviceIdType.MESH
BF = jnp.bfloat16
F32 = jnp.float32
NT = (((1,), (1,)), ((), ()))

NX, NZ = 4, 8
SH = 16
PAIR = 2 * SH
CHUNK = NX * PAIR
TILES = 8

ORDER = (
    ('own',), ('y',), ('x0', 'T', 0), ('x0', 'T', 1), ('z', 1, 'T0'), ('z', 2, 'T0'), ('z', 1, 'C'), ('z', 2, 'C'),
    ('x0', 'C', 0), ('x0', 'C', 1), ('x0b', 'T'), ('z', 1, 'T1'), ('z', 2, 'T1'), ('x', 1, 0), ('x', 1, 1),
    ('z', 1, 'T2'), ('z', 2, 'T2'), ('x', 2, 0), ('x', 2, 1), ('z', 3, 'T0'), ('z', 4, 'T0'), ('x0b', 'C'), ('F', 0),
    ('xb', 1), ('z', 3, 'C'), ('z', 4, 'C'), ('xb', 2), ('G', 0), ('z', 1, 'T3'), ('z', 2, 'T3'), ('F', 1),
    ('x', 3, 0), ('x', 3, 1), ('F', 2), ('z', 3, 'T1'), ('z', 4, 'T1'), ('G', 1), ('H', 0), ('x', 4, 0), ('x', 4, 1),
    ('G', 2), ('z', 3, 'T2'), ('z', 4, 'T2'), ('xb', 3), ('xb', 4), ('z', 5, 'T0'), ('z', 6, 'T0'), ('H', 1),
    ('z', 5, 'C'), ('z', 6, 'C'), ('I', 0), ('J', 0), ('z', 3, 'T3'), ('z', 4, 'T3'), ('F', 3), ('x', 5, 0),
    ('x', 5, 1), ('H', 2), ('z', 5, 'T1'), ('z', 6, 'T1'), ('F', 4), ('x', 6, 0), ('x', 6, 1), ('I', 1), ('G', 3),
    ('z', 5, 'T2'), ('z', 6, 'T2'), ('K', 0), ('I', 2), ('G', 4), ('z', 7, 'T0'), ('xb', 5), ('J', 1), ('z', 7, 'C'),
    ('xb', 6), ('J', 2), ('H', 3), ('z', 5, 'T3'), ('z', 6, 'T3'), ('L', 0), ('F', 5), ('z', 7, 'T1'), ('K', 1),
    ('F', 6), ('z', 7, 'T2'), ('M', 0), ('H', 4), ('z', 7, 'T3'), ('x', 7, 0), ('x', 7, 1), ('G', 5), ('I', 3),
    ('K', 2), ('G', 6), ('J', 3), ('L', 1), ('I', 4), ('xb', 7), ('F', 7), ('J', 4), ('M', 1), ('L', 2), ('H', 5),
    ('G', 7), ('K', 3), ('K', 4), ('M', 2), ('H', 6), ('I', 5), ('L', 3), ('J', 5), ('L', 4), ('M', 3), ('H', 7),
    ('K', 5), ('M', 4), ('I', 6), ('J', 6), ('I', 7), ('L', 5), ('J', 7), ('K', 6), ('ht',), ('M', 5), ('W', 0),
    ('W', 1), ('K', 7), ('W', 2), ('L', 6), ('W', 3), ('W', 4), ('M', 6), ('L', 7), ('W', 5), ('W', 6), ('M', 7),
    ('W', 7), ('N',),
)


def distance(k):
    return (k + 1) // 2


class Step:
    def __init__(self, refs):
        (self.tok_in, self.cot_in, self.wg_in, self.wu_in, self.wd_in,
         self.out, self.og, self.ou, self.od,
         self.tok, self.cot, self.wg, self.wu, self.wd, self.part, self.s1, self.s2, self.back,
         self.tot, self.b1, self.b2, self.r1, self.r2, self.by, self.ry, self.bz, self.rz,
         self.vg, self.vu, self.vd, self.ht, self.send_sem, self.recv_sem, self.local_sem) = refs
        hid, mod = lax.axis_index("hid"), lax.axis_index("mod")
        self.x, self.yl, self.z = hid // 16, (hid // 8) % 2, hid % 8
        self.yh, self.c = mod // 2, mod % 2
        self.ids = {}
        self.sent = []
        self.n_local = 0
        self.local = []
        half = self.tok.shape[1] // 2
        self.half = (pl.ds(0, half), pl.ds(half, half))

    def dev(self, dx=0, dz=0, yl=None, yh=None, c=None):
        x = lax.rem(self.x + (dx + NX), NX)
        z = lax.rem(self.z + (dz + NZ), NZ)
        yl = self.yl if yl is None else yl
        yh = self.yh if yh is None else yh
        c = self.c if c is None else c
        return (x * 16 + yl * 8 + z, yh * 2 + c)

    def zchunk(self, k):
        d = distance(k) if k % 2 == 0 else -distance(k)
        return lax.rem(self.z + (d + NZ), NZ)

    def xblock(self, dx):
        return lax.rem(self.x + (dx + NX), NX)

    def rows(self, k, dx=None, y=None):
        base = self.zchunk(k) * CHUNK
        if dx is None:
            return pl.ds(pl.multiple_of(base, CHUNK), CHUNK)
        base = base + self.xblock(dx) * PAIR
        if y is None:
            return pl.ds(pl.multiple_of(base, PAIR), PAIR)
        return pl.ds(pl.multiple_of(base + y * SH, SH), SH)

    def quarter(self, k, c, yh):
        return pl.ds(pl.multiple_of(self.zchunk(k) * CHUNK + c * 64 + yh * 32, 32), 32)

    def sem(self, key):
        return self.ids.setdefault(key, len(self.ids))

    def send(self, key, src, dst, dev):
        i = self.sem(key)
        cp = pltpu.make_async_remote_copy(src_ref=src, dst_ref=dst, send_sem=self.send_sem.at[i],
                                          recv_sem=self.recv_sem.at[i], device_id=dev, device_id_type=MESH)
        cp.start()
        self.sent.append(cp)

    def wait(self, key, dst, dev):
        i = self.sem(key)
        pltpu.make_async_remote_copy(src_ref=dst, dst_ref=dst, send_sem=self.send_sem.at[i],
                                     recv_sem=self.recv_sem.at[i], device_id=dev, device_id_type=MESH).wait_recv()

    def fetch(self, src, dst):
        cp = pltpu.make_async_copy(src, dst, self.local_sem.at[self.n_local])
        self.n_local += 1
        cp.start()
        return cp

    def xd(self, q):
        return self.dev(dx=1 if q == 0 else -1)

    def zd(self, q):
        return self.dev(dz=1 if q == 0 else -1)

    def arr(self, a):
        return self.tok if a == "T" else self.cot

    def begin(self):
        own = self.rows(0, 0, self.yl)
        first = (self.fetch(self.tok_in, self.tok.at[own]), self.fetch(self.cot_in, self.cot.at[own]))
        self.weights = (self.fetch(self.wg_in, self.wg), self.fetch(self.wu_in, self.wu), self.fetch(self.wd_in, self.wd))
        bar = pltpu.get_barrier_semaphore()
        peers = [self.xd(0), self.xd(1), self.dev(yl=1 - self.yl), self.dev(yh=1 - self.yh), self.dev(c=1 - self.c)]
        peers += [self.dev(dz=d) for d in (1, -1, 2, -2, 3, -3, 4)]
        for p in peers:
            pl.semaphore_signal(bar, inc=1, device_id=p, device_id_type=MESH)
        pl.semaphore_wait(bar, len(peers))
        for cp in first:
            cp.wait()

    def plane(self, a, y, part):
        r = self.arr(a).at[self.rows(0, 0, y)]
        for q in (0, 1):
            self.send(("x0", a, q, part), r, r, self.xd(q))
        for q in (0, 1):
            self.send(("z", 1 + q, a + "o", part), r, r, self.zd(q))

    def own(self):
        for a in "TC":
            r = self.arr(a).at[self.rows(0, 0, self.yl)]
            self.send(("y", a), r, r, self.dev(yl=1 - self.yl))
        for a in "TC":
            self.plane(a, self.yl, 0)

    def y(self):
        for a in "TC":
            self.wait(("y", a), self.arr(a).at[self.rows(0, 0, 1 - self.yl)], self.dev(yl=1 - self.yl))
            self.plane(a, 1 - self.yl, 1)

    def x0(self, a, q):
        dx = -1 if q == 0 else 1
        for part, y in ((0, self.yl), (1, 1 - self.yl)):
            self.wait(("x0", a, q, part), self.arr(a).at[self.rows(0, dx, y)], self.xd(1 - q))
        r = self.arr(a).at[self.rows(0, dx)]
        h = self.arr(a).at[self.rows(0, dx), self.half[q]]
        self.send(("x0b", a, q), h, h, self.xd(q))
        if a == "T":
            for p in (0, 1):
                self.send(("z", 1 + p, "T%d" % (1 + q), 0), r, r, self.zd(p))

    def x0b(self, a):
        for q in (0, 1):
            self.wait(("x0b", a, q), self.arr(a).at[self.rows(0, 2), self.half[q]], self.xd(1 - q))
        if a == "T":
            r = self.tok.at[self.rows(0, 2)]
            for p in (0, 1):
                self.send(("z", 1 + p, "T3", 0), r, r, self.zd(p))

    def zin(self, k, p):
        d = 0 if k % 2 else 1
        a = self.arr(p[0])
        dx = {"C": 0, "T0": 0, "T1": -1, "T2": 1, "T3": 2}[p]
        r = a.at[self.rows(k, dx)]
        if k == 7:
            for q in (0, 1):
                self.wait(("z", 7, p, q), a.at[self.rows(k, dx), self.half[q]], self.zd(1 - q))
        elif k <= 2 and dx == 0:
            for part, y in ((0, self.yl), (1, 1 - self.yl)):
                self.wait(("z", k, p[0] + "o", part), a.at[self.rows(k, dx, y)], self.zd(1 - d))
        else:
            self.wait(("z", k, p, 0), r, self.zd(1 - d))
        if k < 5:
            self.send(("z", k + 2, p, 0), r, r, self.zd(d))
        elif k < 7:
            h = a.at[self.rows(k, dx), self.half[d]]
            self.send(("z", 7, p, d), h, h, self.zd(d))
        if p == "C":
            for q in (0, 1):
                self.send(("x", k, q), r, r, self.xd(q))

    def xin(self, k, q):
        dx = -1 if q == 0 else 1
        self.wait(("x", k, q), self.cot.at[self.rows(k, dx)], self.xd(1 - q))
        h = self.cot.at[self.rows(k, dx), self.half[q]]
        self.send(("xb", k, q), h, h, self.xd(q))

    def xb(self, k):
        for q in (0, 1):
            self.wait(("xb", k, q), self.cot.at[self.rows(k, 2), self.half[q]], self.xd(1 - q))

    def F(self, k):
        if k == 0:
            for cp in self.weights:
                cp.wait()
        r = self.rows(k)
        t = self.tok[r, :]
        self.part[k, 0] = jnp.dot(t, self.wg[...], preferred_element_type=F32)
        self.part[k, 1] = jnp.dot(t, self.wu[...], preferred_element_type=F32)
        self.part[k, 2] = lax.dot_general(self.cot[r, :], self.wd[...], NT, preferred_element_type=F32)
        other = pl.ds(pl.multiple_of((1 - self.c) * 64, 64), 64)
        self.send(("s1", k), self.part.at[k, :, other, :], self.s1.at[k], self.dev(c=1 - self.c))

    def G(self, k):
        self.wait(("s1", k), self.s1.at[k], self.dev(c=1 - self.c))
        there = pl.ds(pl.multiple_of((1 - self.yh) * 32, 32), 32)
        mine = pl.ds(pl.multiple_of(self.c * 64 + (1 - self.yh) * 32, 32), 32)
        self.part[k, :, mine, :] = self.part[k, :, mine, :] + self.s1[k, :, there, :]
        self.send(("s2", k), self.part.at[k, :, mine, :], self.s2.at[k], self.dev(yh=1 - self.yh))

    def H(self, k):
        self.wait(("s2", k), self.s2.at[k], self.dev(yh=1 - self.yh))
        here = pl.ds(pl.multiple_of(self.yh * 32, 32), 32)
        mine = pl.ds(pl.multiple_of(self.c * 64 + self.yh * 32, 32), 32)
        gate, up, grad = (self.part[k, i, mine, :] + self.s1[k, i, here, :] + self.s2[k, i] for i in range(3))
        s = jax.nn.sigmoid(gate)
        a = gate * s
        r = self.quarter(k, self.c, self.yh)
        self.back[0, r, :] = (a * up).astype(BF)
        self.back[1, r, :] = (grad * up * (s * (1.0 + gate * (1.0 - s)))).astype(BF)
        self.back[2, r, :] = (grad * a).astype(BF)
        b = self.back.at[:, r, :]
        self.send(("s3", k), b, b, self.dev(yh=1 - self.yh))
        self.send(("s4", k, 0), b, b, self.dev(c=1 - self.c))

    def I(self, k):
        b = self.back.at[:, self.quarter(k, self.c, 1 - self.yh), :]
        self.wait(("s3", k), b, self.dev(yh=1 - self.yh))
        self.send(("s4", k, 1), b, b, self.dev(c=1 - self.c))

    def J(self, k):
        for i, yh in ((0, self.yh), (1, 1 - self.yh)):
            self.wait(("s4", k, i), self.back.at[:, self.quarter(k, 1 - self.c, yh), :], self.dev(c=1 - self.c))
        r = self.rows(k)
        self.tot[k] = lax.dot_general(
            self.back[1, r, :], self.wg[...], NT, preferred_element_type=F32
        ) + lax.dot_general(self.back[2, r, :], self.wu[...], NT, preferred_element_type=F32)
        self.b1[k] = self.tot[k, self.block(2), :].astype(BF)
        for q in (0, 1):
            self.send(("r1", k, q), self.b1.at[k, :, self.half[q]], self.r1.at[k, q], self.xd(q))

    def block(self, dx):
        return pl.ds(pl.multiple_of(self.xblock(dx) * PAIR, PAIR), PAIR)

    def K(self, k):
        for q in (0, 1):
            self.wait(("r1", k, q), self.r1.at[k, q], self.xd(1 - q))
            b = self.block(1 if q == 0 else -1)
            self.b2[k, q, :, self.half[q]] = (self.tot[k, b, self.half[q]] + self.r1[k, q].astype(F32)).astype(BF)
            self.b2[k, q, :, self.half[1 - q]] = self.tot[k, b, self.half[1 - q]].astype(BF)
            self.send(("r2", k, q), self.b2.at[k, q], self.r2.at[k, q], self.xd(q))

    def L(self, k):
        for q in (0, 1):
            self.wait(("r2", k, q), self.r2.at[k, q], self.xd(1 - q))
        b = self.block(0)
        self.tot[k, b, :] = self.tot[k, b, :] + self.r2[k, 0].astype(F32) + self.r2[k, 1].astype(F32)
        self.by[k] = self.tot[k, self.yrows(1 - self.yl), :].astype(BF)
        self.send(("ry", k), self.by.at[k], self.ry.at[k], self.dev(yl=1 - self.yl))

    def yrows(self, y):
        return pl.ds(pl.multiple_of(self.xblock(0) * PAIR + y * SH, SH), SH)

    def M(self, k):
        self.wait(("ry", k), self.ry.at[k], self.dev(yl=1 - self.yl))
        s = self.tot[k, self.yrows(self.yl), :] + self.ry[k].astype(F32)
        if k == 0:
            self.tot[k, self.yrows(self.yl), :] = s
        else:
            self.bz[k] = s.astype(BF)
            d = distance(k) if k % 2 == 0 else -distance(k)
            self.send(("rz", k), self.bz.at[k], self.rz.at[k], self.dev(dz=d))

    def N(self):
        s = self.tot[0, self.yrows(self.yl), :]
        for k in range(1, 8):
            d = distance(k) if k % 2 == 0 else -distance(k)
            self.wait(("rz", k), self.rz.at[k], self.dev(dz=-d))
            s = s + self.rz[k].astype(F32)
        self.out[...] = s.astype(BF)

    def turn(self):
        self.ht[...] = self.back[0].T

    def W(self, j):
        n = self.tok.shape[1] // TILES
        cs = pl.ds(j * n, n)
        lt = self.tok[:, cs].T
        self.vg[cs, :] = jnp.dot(lt, self.back[1], preferred_element_type=F32).astype(BF)
        self.vu[cs, :] = jnp.dot(lt, self.back[2], preferred_element_type=F32).astype(BF)
        self.vd[:, cs] = jnp.dot(self.ht[...], self.cot[:, cs], preferred_element_type=F32).astype(BF)
        self.local.append(self.fetch(self.vg.at[cs, :], self.og.at[cs, :]))
        self.local.append(self.fetch(self.vu.at[cs, :], self.ou.at[cs, :]))
        self.local.append(self.fetch(self.vd.at[:, cs], self.od.at[:, cs]))

    def finish(self):
        for cp in self.sent:
            cp.wait_send()
        for cp in self.local:
            cp.wait()


NAMES = {"z": "zin", "x": "xin", "ht": "turn"}


def kernel(*refs):
    step = Step(refs)
    step.begin()
    for name, *args in ORDER:
        getattr(step, NAMES.get(name, name))(*args)
    step.finish()


def shards(tokens, grad_output, gate_weight, up_weight, down_weight):
    d, f = gate_weight.shape
    n = NZ * CHUNK
    anywhere = pl.BlockSpec(memory_space=pl.ANY)
    vmem = pltpu.VMEM
    return pl.pallas_call(
        kernel,
        out_shape=(
            jax.ShapeDtypeStruct((SH, d), BF),
            jax.ShapeDtypeStruct((d, f), BF),
            jax.ShapeDtypeStruct((d, f), BF),
            jax.ShapeDtypeStruct((f, d), BF),
        ),
        in_specs=[anywhere] * 5,
        out_specs=(pl.BlockSpec(memory_space=vmem), anywhere, anywhere, anywhere),
        scratch_shapes=[
            vmem((n, d), BF), vmem((n, d), BF),
            vmem((d, f), BF), vmem((d, f), BF), vmem((f, d), BF),
            vmem((NZ, 3, CHUNK, f), F32), vmem((NZ, 3, 64, f), F32), vmem((NZ, 3, 32, f), F32),
            vmem((3, n, f), BF),
            vmem((NZ, CHUNK, d), F32),
            vmem((NZ, PAIR, d), BF), vmem((NZ, 2, PAIR, d), BF),
            vmem((NZ, 2, PAIR, d // 2), BF), vmem((NZ, 2, PAIR, d), BF),
            vmem((NZ, SH, d), BF), vmem((NZ, SH, d), BF), vmem((NZ, SH, d), BF), vmem((NZ, SH, d), BF),
            vmem((d, f), BF), vmem((d, f), BF), vmem((f, d), BF), vmem((f, n), BF),
            pltpu.SemaphoreType.DMA((200,)), pltpu.SemaphoreType.DMA((200,)), pltpu.SemaphoreType.DMA((5 + 3 * TILES,)),
        ],
        compiler_params=pltpu.CompilerParams(collective_id=0, has_side_effects=True, vmem_limit_bytes=62 << 20),
        cost_estimate=pl.CostEstimate(flops=16 * n * d * f, bytes_accessed=12 * d * f, transcendentals=n * f),
    )(tokens, grad_output, gate_weight, up_weight, down_weight)


def solution(mesh):
    placed = (P("hid", "mod"), P("hid", "mod"), P("mod", "hid"), P("mod", "hid"), P("hid", "mod"))
    return jax.shard_map(
        shards,
        mesh=mesh,
        in_specs=placed,
        out_specs=(P("hid", "mod"), P("mod", "hid"), P("mod", "hid"), P("hid", "mod")),
        check_vma=False,
    )
```

time: 1090 us -> 144 us (0.13)
  the two profiles are of different devices: /device:TPU:16 before, /device:TPU:1 now
where the time goes in v1:
time: 144 us; the launch traced here: 142 us
  Pallas kernels  126 us (88%)
  local copies, waits for them, and re-layouts  16.2 us (11%)
    pallas_call x1, Pallas kernels, shards(): pl.pallas_call(kernel, out_shape=(jax.ShapeDtypeStruct((SH, d), BF), jax....  126 us
    unnamed x10, local copies, waits for them, and re-layouts  9.94 us
    pallas_call x2, local copies, waits for them, and re-layouts, shards(): pl.pallas_call(kernel, out_shape=(jax.ShapeDtypeStruct((SH, d), BF), jax....  6.28 us

profile of v1, /device:TPU:1, one launch (start us, length us, event | category | flops | bytes accessed | tf_op | source)
XLA Modules:
  0.0 142.4 jit_solution(11976252632764258503)
XLA Ops:
  0.6 0.0 copy-start.1
  0.6 3.9 %copy.9.refs_2_ = bf16[2048,448]{1,0:T(8,128)(2,1)} copy(bf16[2048,448]{0,1:T(8,128)(2,1)} %param.7) | data formatting | bytes 3670016 | tf_op args[2]
  4.6 0.0 copy-done.1
  4.6 2.4 %copy.10.refs_3_ = bf16[2048,448]{1,0:T(8,128)(2,1)} copy(bf16[2048,448]{0,1:T(8,128)(2,1)S(1)} %copy-done.1) | data formatting | bytes 3670016 | tf_op args[3]
  7.0 125.5 %shard_map.84 = (bf16[16,2048]{1,0:T(8,128)(2,1)}, bf16[2048,448]{1,0:T(8,128)(2,1)}, bf16[2048,448]{1,0:T(8,128)(2,1)}, bf16[448,2048]{1,0:T(8,128)(2,1)}) custom-call(bf16[16,2048]{1,0:T(8,128)(2,1)} %refs_0_.1, bf16[16,2048]{1,0:T(8,128)(2,1)} %refs_1_.1, bf16[2048,448]{1,0:T(8,128)(2,1)} %copy.9.refs_2_, bf16[2048,448]{1,0:T(8,128)(2,1)} %copy.10.refs_3_, ...), custom_call_target="tpu_custom_call" | custom-call | flops 15032385536 | bytes 11010048 | tf_op jit(solution)/shard_map/pallas_call | solution.py:329
  132.5 0.0 copy-start
  132.6 4.0 %copy.11 = bf16[2048,448]{0,1:T(8,128)(2,1)} copy(bf16[2048,448]{1,0:T(8,128)(2,1)} %get-tuple-element.5) | data formatting | bytes 3670016 | tf_op jit(solution)/shard_map/pallas_call | solution.py:329
  136.6 0.0 copy-done
  136.6 0.0 copy-start.2
  136.6 2.3 %copy.12 = bf16[2048,448]{0,1:T(8,128)(2,1)} copy(bf16[2048,448]{1,0:T(8,128)(2,1)S(1)} %copy-done) | data formatting | bytes 3670016 | tf_op jit(solution)/shard_map/pallas_call | solution.py:329
  138.8 0.0 copy-done.2
  138.8 0.6 copy.15
  139.5 2.9 %copy.16 = bf16[448,2048]{1,0:T(8,128)(2,1)} copy(bf16[448,2048]{1,0:T(8,128)(2,1)} %get-tuple-element.15) | data formatting | bytes 3670016
Async XLA Ops:
  0.6 4.0 %copy-start.1 = (bf16[2048,448]{0,1:T(8,128)(2,1)S(1)}, bf16[2048,448]{0,1:T(8,128)(2,1)}, u32[]{:S(2)}) copy-start(bf16[2048,448]{0,1:T(8,128)(2,1)} %param.8) | copy-start | bytes 5505028
  132.5 4.0 %copy-start = (bf16[2048,448]{1,0:T(8,128)(2,1)S(1)}, bf16[2048,448]{1,0:T(8,128)(2,1)}, u32[]{:S(2)}) copy-start(bf16[2048,448]{1,0:T(8,128)(2,1)} %get-tuple-element.6) | copy-start | bytes 5505028
  136.6 2.3 %copy-start.2 = (bf16[16,2048]{1,0:T(8,128)(2,1)S(1)}, bf16[16,2048]{1,0:T(8,128)(2,1)}, u32[]{:S(2)}) copy-start(bf16[16,2048]{1,0:T(8,128)(2,1)} %get-tuple-element.12) | copy-start | bytes 196612

commit v2 on v1

v2 whole, which is shorter than its diff:
```python
import functools

import jax
import jax.numpy as jnp
from jax import lax
from jax.experimental import pallas as pl
from jax.experimental.pallas import tpu as pltpu
from jax.sharding import PartitionSpec as P

MESH = pl.DeviceIdType.MESH
BF = jnp.bfloat16
F32 = jnp.float32
NT = (((1,), (1,)), ((), ()))

NX, NZ = 4, 8
SH = 16
PAIR = 2 * SH
CHUNK = NX * PAIR
TILES = 8
ZC = ()
DIRECT = (7,)
FAR = (5, 6, 7)
COPIES = 2

ORDER = (
    ('own',), ('y',), ('x0', 'T', 0), ('x0', 'T', 1), ('z', 1, 'C'), ('z', 2, 'C'), ('z', 1, 'T0'), ('z', 2, 'T0'),
    ('x0', 'C', 0), ('x0', 'C', 1), ('x0b', 'T'), ('z', 1, 'T1'), ('z', 2, 'T1'), ('x', 1, 0), ('x', 1, 1),
    ('z', 1, 'T2'), ('z', 2, 'T2'), ('x', 2, 0), ('x', 2, 1), ('z', 3, 'C'), ('z', 4, 'C'), ('x0b', 'C'), ('F', 0),
    ('xb', 1), ('z', 3, 'T0'), ('z', 4, 'T0'), ('xb', 2), ('G', 0), ('z', 1, 'T3'), ('z', 2, 'T3'), ('F', 2),
    ('F', 1), ('x', 3, 0), ('z', 3, 'T1'), ('z', 4, 'T1'), ('x', 4, 0), ('G', 2), ('x', 4, 1), ('x', 3, 1), ('H', 0),
    ('G', 1), ('z', 3, 'T2'), ('z', 4, 'T2'), ('J', 0), ('xb', 4), ('xb', 3), ('z', 5, 'C'), ('z', 6, 'C'), ('H', 2),
    ('K', 0), ('z', 5, 'T0'), ('z', 6, 'T0'), ('J', 2), ('x', 5, 1), ('x', 5, 0), ('z', 3, 'T3'), ('F', 3),
    ('z', 4, 'T3'), ('H', 1), ('F', 4), ('G', 3), ('z', 5, 'T1'), ('z', 6, 'T1'), ('x', 6, 0), ('J', 1), ('L', 0),
    ('z', 5, 'T2'), ('z', 6, 'T2'), ('G', 4), ('x', 6, 1), ('K', 2), ('z', 7, 'C'), ('xb', 5), ('z', 7, 'T0'),
    ('H', 3), ('xb', 6), ('K', 1), ('z', 5, 'T3'), ('z', 6, 'T3'), ('F', 5), ('z', 7, 'T1'), ('M', 0), ('J', 3),
    ('z', 7, 'T2'), ('G', 5), ('F', 6), ('z', 7, 'T3'), ('x', 7, 1), ('x', 7, 0), ('L', 2), ('H', 4), ('G', 6),
    ('J', 4), ('L', 1), ('K', 3), ('H', 5), ('xb', 7), ('F', 7), ('J', 5), ('M', 2), ('G', 7), ('K', 4), ('L', 3),
    ('H', 6), ('M', 1), ('K', 5), ('J', 6), ('L', 4), ('H', 7), ('M', 3), ('L', 5), ('J', 7), ('M', 4), ('K', 6),
    ('ht',), ('W', 0), ('W', 1), ('W', 2), ('W', 3), ('W', 4), ('L', 7), ('W', 5), ('W', 6), ('L', 6), ('W', 7),
    ('N',),
)


def distance(k):
    return (k + 1) // 2


def offset(k):
    return distance(k) if k % 2 == 0 else -distance(k)


class Step:
    def __init__(self, refs):
        (self.tok_in, self.cot_in, self.wg_in, self.wu_in, self.wd_in,
         self.out, self.og, self.ou, self.od,
         self.tok, self.cot, self.wg, self.wu, self.wd, self.part, self.s1, self.g2, self.s2, self.back,
         self.tot, self.b1, self.b2, self.r1, self.r2, self.by, self.ry, self.bz, self.rz,
         self.vg, self.vu, self.vd, self.ht, self.send_sem, self.recv_sem, self.local_sem) = refs
        hid, mod = lax.axis_index("hid"), lax.axis_index("mod")
        self.x, self.yl, self.z = hid // 16, (hid // 8) % 2, hid % 8
        self.yh, self.c = mod // 2, mod % 2
        self.ids = {}
        self.sent = []
        self.n_local = 0
        self.local = []
        half = self.tok.shape[1] // 2
        self.half = (pl.ds(0, half), pl.ds(half, half))

    def dev(self, dx=0, dz=0, yl=None, yh=None, c=None):
        x = lax.rem(self.x + (dx + NX), NX)
        z = lax.rem(self.z + (dz + NZ), NZ)
        yl = self.yl if yl is None else yl
        yh = self.yh if yh is None else yh
        c = self.c if c is None else c
        return (x * 16 + yl * 8 + z, yh * 2 + c)

    def zchunk(self, k):
        return lax.rem(self.z + (offset(k) + NZ), NZ)

    def xblock(self, dx):
        return lax.rem(self.x + (dx + NX), NX)

    def rows(self, k, dx=None, y=None):
        base = self.zchunk(k) * CHUNK
        if dx is None:
            return pl.ds(pl.multiple_of(base, CHUNK), CHUNK)
        base = base + self.xblock(dx) * PAIR
        if y is None:
            return pl.ds(pl.multiple_of(base, PAIR), PAIR)
        return pl.ds(pl.multiple_of(base + y * SH, SH), SH)

    def side(self, k, c):
        return pl.ds(pl.multiple_of(self.zchunk(k) * CHUNK + c * 64, 64), 64)

    def sem(self, key):
        return self.ids.setdefault(key, len(self.ids))

    def send(self, key, src, dst, dev):
        i = self.sem(key)
        cp = pltpu.make_async_remote_copy(src_ref=src, dst_ref=dst, send_sem=self.send_sem.at[i],
                                          recv_sem=self.recv_sem.at[i], device_id=dev, device_id_type=MESH)
        cp.start()
        self.sent.append(cp)

    def wait(self, key, dst, dev):
        i = self.sem(key)
        pltpu.make_async_remote_copy(src_ref=dst, dst_ref=dst, send_sem=self.send_sem.at[i],
                                     recv_sem=self.recv_sem.at[i], device_id=dev, device_id_type=MESH).wait_recv()

    def fetch(self, src, dst):
        cp = pltpu.make_async_copy(src, dst, self.local_sem.at[self.n_local])
        self.n_local += 1
        cp.start()
        return cp

    def xd(self, q):
        return self.dev(dx=1 if q == 0 else -1)

    def zd(self, q):
        return self.dev(dz=1 if q == 0 else -1)

    def arr(self, a):
        return self.tok if a == "T" else self.cot

    def begin(self):
        own = self.rows(0, 0, self.yl)
        first = (self.fetch(self.tok_in, self.tok.at[own]), self.fetch(self.cot_in, self.cot.at[own]))
        self.weights = (self.fetch(self.wg_in, self.wg), self.fetch(self.wu_in, self.wu), self.fetch(self.wd_in, self.wd))
        bar = pltpu.get_barrier_semaphore()
        peers = [self.xd(0), self.xd(1), self.dev(yl=1 - self.yl), self.dev(yh=1 - self.yh), self.dev(c=1 - self.c)]
        peers += [self.zd(0), self.zd(1)]
        for p in peers:
            pl.semaphore_signal(bar, inc=1, device_id=p, device_id_type=MESH)
        pl.semaphore_wait(bar, len(peers))
        for cp in first:
            cp.wait()

    def plane(self, to, a, y, part):
        r = self.arr(a).at[self.rows(0, 0, y)]
        for q in (0, 1):
            if to == "x":
                self.send(("x0", a, q, part), r, r, self.xd(q))
            else:
                self.send(("z", 1 + q, a + "o", part), r, r, self.zd(q))

    def own(self):
        for a in "TC":
            r = self.arr(a).at[self.rows(0, 0, self.yl)]
            self.send(("y", a), r, r, self.dev(yl=1 - self.yl))
        for to, a in (("x", "T"), ("x", "C"), ("z", "C"), ("z", "T")):
            self.plane(to, a, self.yl, 0)

    def y(self):
        for a in "TC":
            self.wait(("y", a), self.arr(a).at[self.rows(0, 0, 1 - self.yl)], self.dev(yl=1 - self.yl))
        for to, a in (("x", "T"), ("x", "C"), ("z", "C"), ("z", "T")):
            self.plane(to, a, 1 - self.yl, 1)

    def x0(self, a, q):
        dx = -1 if q == 0 else 1
        for part, y in ((0, self.yl), (1, 1 - self.yl)):
            self.wait(("x0", a, q, part), self.arr(a).at[self.rows(0, dx, y)], self.xd(1 - q))
        r = self.arr(a).at[self.rows(0, dx)]
        h = self.arr(a).at[self.rows(0, dx), self.half[q]]
        self.send(("x0b", a, q), h, h, self.xd(q))
        if a == "T":
            for p in (0, 1):
                self.send(("z", 1 + p, "T%d" % (1 + q), 0), r, r, self.zd(p))

    def x0b(self, a):
        for q in (0, 1):
            self.wait(("x0b", a, q), self.arr(a).at[self.rows(0, 2), self.half[q]], self.xd(1 - q))
        if a == "T":
            r = self.tok.at[self.rows(0, 2)]
            for p in (0, 1):
                self.send(("z", 1 + p, "T3", 0), r, r, self.zd(p))

    def zin(self, k, p):
        d = 0 if k % 2 else 1
        a = self.arr(p[0])
        dx = {"": 0, "0": 0, "1": -1, "2": 1, "3": 2}[p[1:]]
        r = a.at[self.rows(k, dx)]
        if k == 7:
            for q in (0, 1):
                self.wait(("z", 7, p, q), a.at[self.rows(k, dx), self.half[q]], self.zd(1 - q))
        elif k <= 2 and dx == 0:
            for part, y in ((0, self.yl), (1, 1 - self.yl)):
                self.wait(("z", k, p[0] + "o", part), a.at[self.rows(k, dx, y)], self.zd(1 - d))
        else:
            self.wait(("z", k, p, 0), r, self.zd(1 - d))
        self.onward(k, p, dx)
        if p == "C" and k not in ZC:
            for q in (0, 1):
                self.send(("x", k, q), r, r, self.xd(q))

    def onward(self, k, p, dx):
        d = 0 if k % 2 else 1
        a = self.arr(p[0])
        if k < 5:
            r = a.at[self.rows(k, dx)]
            self.send(("z", k + 2, p, 0), r, r, self.zd(d))
        elif k < 7:
            h = a.at[self.rows(k, dx), self.half[d]]
            self.send(("z", 7, p, d), h, h, self.zd(d))

    def xin(self, k, q):
        dx = -1 if q == 0 else 1
        self.wait(("x", k, q), self.cot.at[self.rows(k, dx)], self.xd(1 - q))
        h = self.cot.at[self.rows(k, dx), self.half[q]]
        self.send(("xb", k, q), h, h, self.xd(q))
        if min(k + 2, 7) in ZC:
            self.onward(k, "C%d" % (1 + q), dx)

    def xb(self, k):
        for q in (0, 1):
            self.wait(("xb", k, q), self.cot.at[self.rows(k, 2), self.half[q]], self.xd(1 - q))
        if min(k + 2, 7) in ZC:
            self.onward(k, "C3", 2)

    def ready(self):
        for cp in self.weights:
            cp.wait()
        self.weights = ()

    def F(self, k):
        self.ready()
        r = self.rows(k)
        t = self.tok[r, :]
        self.part[k, 0] = lax.dot_general(t, self.wg[...], NT, preferred_element_type=F32)
        self.part[k, 1] = lax.dot_general(t, self.wu[...], NT, preferred_element_type=F32)
        self.part[k, 2] = lax.dot_general(self.cot[r, :], self.wd[...], NT, preferred_element_type=F32)
        other = pl.ds(pl.multiple_of((1 - self.c) * 64, 64), 64)
        self.send(("s1", k), self.part.at[k, :, other, :], self.s1.at[k], self.dev(c=1 - self.c))

    def G(self, k):
        self.wait(("s1", k), self.s1.at[k], self.dev(c=1 - self.c))
        mine = pl.ds(pl.multiple_of(self.c * 64, 64), 64)
        for i in range(3):
            total = self.part[k, i, mine, :] + self.s1[k, i]
            self.s1[k, i] = total
            self.g2[k, i] = total.astype(BF)
        self.send(("s2", k), self.g2.at[k], self.s2.at[k], self.dev(yh=1 - self.yh))

    def H(self, k):
        self.wait(("s2", k), self.s2.at[k], self.dev(yh=1 - self.yh))
        gate, up, grad = (self.s1[k, i] + self.s2[k, i].astype(F32) for i in range(3))
        s = jax.nn.sigmoid(gate)
        a = gate * s
        r = self.side(k, self.c)
        self.back[0, r, :] = (a * up).astype(BF)
        self.back[1, r, :] = (grad * up * (s * (1.0 + gate * (1.0 - s)))).astype(BF)
        self.back[2, r, :] = (grad * a).astype(BF)
        b = self.back.at[:, r, :]
        self.send(("s4", k), b, b, self.dev(c=1 - self.c))

    def J(self, k):
        self.wait(("s4", k), self.back.at[:, self.side(k, 1 - self.c), :], self.dev(c=1 - self.c))
        r = self.rows(k)
        self.tot[k] = jnp.dot(self.back[1, r, :], self.wg[...], preferred_element_type=F32) + jnp.dot(
            self.back[2, r, :], self.wu[...], preferred_element_type=F32
        )
        self.b1[k] = self.tot[k, self.block(2), :].astype(BF)
        if k in DIRECT:
            self.send(("r1", k), self.b1.at[k], self.r1.at[k], self.dev(dx=2))
            for q in (0, 1):
                self.b2[k, q] = self.tot[k, self.block(1 if q == 0 else -1), :].astype(BF)
                self.send(("r2", k, q), self.b2.at[k, q], self.r2.at[k, q], self.xd(q))
        else:
            for q in (0, 1):
                self.send(("r1", k, q), self.b1.at[k, :, self.half[q]], self.r1.at[k, :, self.half[q]], self.xd(q))

    def block(self, dx):
        return pl.ds(pl.multiple_of(self.xblock(dx) * PAIR, PAIR), PAIR)

    def K(self, k):
        for q in (0, 1):
            h, o = self.half[q], self.half[1 - q]
            self.wait(("r1", k, q), self.r1.at[k, :, h], self.xd(1 - q))
            b = self.block(1 if q == 0 else -1)
            self.b2[k, q, :, h] = (self.tot[k, b, h] + self.r1[k, :, h].astype(F32)).astype(BF)
            self.b2[k, q, :, o] = self.tot[k, b, o].astype(BF)
            self.send(("r2", k, q), self.b2.at[k, q], self.r2.at[k, q], self.xd(q))

    def L(self, k):
        for q in (0, 1):
            self.wait(("r2", k, q), self.r2.at[k, q], self.xd(1 - q))
        b = self.block(0)
        s = self.tot[k, b, :] + self.r2[k, 0].astype(F32) + self.r2[k, 1].astype(F32)
        if k in DIRECT:
            self.wait(("r1", k), self.r1.at[k], self.dev(dx=2))
            s = s + self.r1[k].astype(F32)
        self.tot[k, b, :] = s
        if k in FAR:
            for i, y in ((0, self.yl), (1, 1 - self.yl)):
                self.bz[k, i] = self.tot[k, self.yrows(y), :].astype(BF)
                self.send(("rz", k, i), self.bz.at[k, i], self.rz.at[k, i], self.dev(dz=offset(k), yl=y))
        else:
            self.by[k] = self.tot[k, self.yrows(1 - self.yl), :].astype(BF)
            self.send(("ry", k), self.by.at[k], self.ry.at[k], self.dev(yl=1 - self.yl))

    def yrows(self, y):
        return pl.ds(pl.multiple_of(self.xblock(0) * PAIR + y * SH, SH), SH)

    def M(self, k):
        self.wait(("ry", k), self.ry.at[k], self.dev(yl=1 - self.yl))
        s = self.tot[k, self.yrows(self.yl), :] + self.ry[k].astype(F32)
        if k == 0:
            self.tot[k, self.yrows(self.yl), :] = s
        else:
            self.bz[k, 0] = s.astype(BF)
            self.send(("rz", k, 0), self.bz.at[k, 0], self.rz.at[k, 0], self.dev(dz=offset(k)))

    def N(self):
        s = self.tot[0, self.yrows(self.yl), :]
        for k in range(1, NZ):
            for i, y in ((0, self.yl), (1, 1 - self.yl))[: 2 if k in FAR else 1]:
                self.wait(("rz", k, i), self.rz.at[k, i], self.dev(dz=-offset(k), yl=y))
                s = s + self.rz[k, i].astype(F32)
        self.out[...] = s.astype(BF)

    def turn(self):
        for i in range(3):
            self.ht[i] = self.back[i].T

    def W(self, j):
        n = self.tok.shape[1] // TILES
        cs = pl.ds(j * n, n)
        for i, a, v, o in ((1, self.tok, self.vg, self.og), (2, self.tok, self.vu, self.ou), (0, self.cot, self.vd, self.od)):
            v[:, cs] = jnp.dot(self.ht[i], a[:, cs], preferred_element_type=F32).astype(BF)
            self.local.append(self.fetch(v.at[:, cs], o.at[:, cs]))

    def finish(self):
        self.ready()
        for cp in self.sent:
            cp.wait_send()
        for cp in self.local:
            cp.wait()


NAMES = {"z": "zin", "x": "xin", "ht": "turn"}


def kernel(*refs):
    step = Step(refs)
    step.begin()
    for name, *args in ORDER:
        getattr(step, NAMES.get(name, name))(*args)
    step.finish()


def hand_over(*refs):
    for src, dst in zip(refs[:4], refs[4:]):
        dst[...] = src[...]


def shards(tokens, grad_output, gate_weight, up_weight, down_weight):
    d, f = gate_weight.shape
    n = NZ * CHUNK
    anywhere = pl.BlockSpec(memory_space=pl.ANY)
    vmem = pltpu.VMEM
    results = pl.pallas_call(
        kernel,
        out_shape=(
            jax.ShapeDtypeStruct((SH, d), BF),
            jax.ShapeDtypeStruct((f, d), BF),
            jax.ShapeDtypeStruct((f, d), BF),
            jax.ShapeDtypeStruct((f, d), BF),
        ),
        in_specs=[anywhere] * 5,
        out_specs=(pl.BlockSpec(memory_space=vmem), anywhere, anywhere, anywhere),
        scratch_shapes=[
            vmem((n, d), BF), vmem((n, d), BF),
            vmem((f, d), BF), vmem((f, d), BF), vmem((f, d), BF),
            vmem((NZ, 3, CHUNK, f), F32), vmem((NZ, 3, 64, f), F32), vmem((NZ, 3, 64, f), BF), vmem((NZ, 3, 64, f), BF),
            vmem((3, n, f), BF),
            vmem((NZ, CHUNK, d), F32),
            vmem((NZ, PAIR, d), BF), vmem((NZ, 2, PAIR, d), BF),
            vmem((NZ, PAIR, d), BF), vmem((NZ, 2, PAIR, d), BF),
            vmem((NZ, SH, d), BF), vmem((NZ, SH, d), BF), vmem((NZ, 2, SH, d), BF), vmem((NZ, 2, SH, d), BF),
            vmem((f, d), BF), vmem((f, d), BF), vmem((f, d), BF), vmem((3, f, n), BF),
            pltpu.SemaphoreType.DMA((200,)), pltpu.SemaphoreType.DMA((200,)), pltpu.SemaphoreType.DMA((5 + 3 * TILES,)),
        ],
        compiler_params=pltpu.CompilerParams(collective_id=0, has_side_effects=True, vmem_limit_bytes=62 << 20),
        cost_estimate=pl.CostEstimate(flops=16 * n * d * f, bytes_accessed=12 * d * f, transcendentals=n * f),
    )(tokens, grad_output, gate_weight.T, up_weight.T, down_weight)
    blocks = [pl.BlockSpec((SH, d), lambda i: (0, 0))] + [pl.BlockSpec((f // COPIES, d), lambda i: (i, 0))] * 3
    grad_tokens, grad_gate, grad_up, grad_down = pl.pallas_call(
        hand_over,
        grid=(COPIES,),
        out_shape=tuple(jax.ShapeDtypeStruct(r.shape, r.dtype) for r in results),
        in_specs=blocks,
        out_specs=tuple(blocks),
    )(*results)
    return grad_tokens, grad_gate.T, grad_up.T, grad_down


def solution(mesh):
    placed = (P("hid", "mod"), P("hid", "mod"), P("mod", "hid"), P("mod", "hid"), P("hid", "mod"))
    return jax.shard_map(
        shards,
        mesh=mesh,
        in_specs=placed,
        out_specs=(P("hid", "mod"), P("mod", "hid"), P("mod", "hid"), P("hid", "mod")),
        check_vma=False,
    )
```

time: 144 us -> 121 us (0.84)
  local copies, waits for them, and re-layouts: 16.2 us -> 0 us
  Pallas kernels: 126 us -> 120 us
    pallas_call x1, Pallas kernels: 126 us -> 115 us  [shards(): pl.pallas_call(kernel, out_shape=(jax.ShapeDtypeStruct((SH, d), BF), jax....]
    unnamed x10 -> x0, local copies, waits for them, and re-layouts: 9.94 us -> none
    pallas_call x2 -> x0, local copies, waits for them, and re-layouts: 6.28 us -> none  [shards(): pl.pallas_call(kernel, out_shape=(jax.ShapeDtypeStruct((SH, d), BF), jax....]
    pallas_call x0 -> x1, Pallas kernels: none -> 4.87 us  [shards(): pl.pallas_call(hand_over, grid=(COPIES,), out_shape=tuple((jax.ShapeDtype...]
where the time goes in v2:
time: 121 us; the launch traced here: 120 us
  Pallas kernels  120 us (99%)
    pallas_call x1, Pallas kernels, shards(): pl.pallas_call(kernel, out_shape=(jax.ShapeDtypeStruct((SH, d), BF), jax....  115 us
    pallas_call x1, Pallas kernels, shards(): pl.pallas_call(hand_over, grid=(COPIES,), out_shape=tuple((jax.ShapeDtype...  4.87 us

profile of v2, /device:TPU:1, one launch (start us, length us, event | category | flops | bytes accessed | tf_op | source)
XLA Modules:
  0.0 120.5 jit_solution(15461755996108342178)
XLA Ops:
  0.6 115.0 %shard_map.84 = (bf16[16,2048]{1,0:T(8,128)(2,1)}, bf16[448,2048]{1,0:T(8,128)(2,1)}, bf16[448,2048]{1,0:T(8,128)(2,1)}, bf16[448,2048]{1,0:T(8,128)(2,1)}) custom-call(bf16[16,2048]{1,0:T(8,128)(2,1)} %refs_0_.1, bf16[16,2048]{1,0:T(8,128)(2,1)} %refs_1_.1, bf16[448,2048]{1,0:T(8,128)(2,1)} %bitcast.4, bf16[448,2048]{1,0:T(8,128)(2,1)} %bitcast.5, ...), custom_call_target="tpu_custom_call" | custom-call | flops 15032385536 | bytes 11010048 | tf_op jit(solution)/shard_map/pallas_call | solution.py:361
  115.6 4.9 %shard_map.85 = (bf16[16,2048]{1,0:T(8,128)(2,1)}, bf16[448,2048]{1,0:T(8,128)(2,1)}, bf16[448,2048]{1,0:T(8,128)(2,1)}, bf16[448,2048]{1,0:T(8,128)(2,1)}) custom-call(bf16[16,2048]{1,0:T(8,128)(2,1)} %get-tuple-element.12.refs_0_, bf16[448,2048]{1,0:T(8,128)(2,1)} %get-tuple-element.13.refs_1_, bf16[448,2048]{1,0:T(8,128)(2,1)} %get-tuple-element.14.refs_2_, ...), custom_call_target="tpu_custom_call" | custom-call | tf_op jit(solution)/shard_map/pallas_call | solution.py:387

commit v3 on v2

--- a/solution.py
+++ b/solution.py
@@ -17,26 +17,27 @@
 PAIR = 2 * SH
 CHUNK = NX * PAIR
 TILES = 8
-ZC = ()
+ZC = (7,)
+TX = (3, 4, 5, 6, 7)
+YF = (0,)
 DIRECT = (7,)
-FAR = (5, 6, 7)
-COPIES = 2
+FAR = (6, 7)
 
 ORDER = (
     ('own',), ('y',), ('x0', 'T', 0), ('x0', 'T', 1), ('z', 1, 'C'), ('z', 2, 'C'), ('z', 1, 'T0'), ('z', 2, 'T0'),
     ('x0', 'C', 0), ('x0', 'C', 1), ('x0b', 'T'), ('z', 1, 'T1'), ('z', 2, 'T1'), ('x', 1, 0), ('x', 1, 1),
     ('z', 1, 'T2'), ('z', 2, 'T2'), ('x', 2, 0), ('x', 2, 1), ('z', 3, 'C'), ('z', 4, 'C'), ('x0b', 'C'), ('F', 0),
-    ('xb', 1), ('z', 3, 'T0'), ('z', 4, 'T0'), ('xb', 2), ('G', 0), ('z', 1, 'T3'), ('z', 2, 'T3'), ('F', 2),
-    ('F', 1), ('x', 3, 0), ('z', 3, 'T1'), ('z', 4, 'T1'), ('x', 4, 0), ('G', 2), ('x', 4, 1), ('x', 3, 1), ('H', 0),
-    ('G', 1), ('z', 3, 'T2'), ('z', 4, 'T2'), ('J', 0), ('xb', 4), ('xb', 3), ('z', 5, 'C'), ('z', 6, 'C'), ('H', 2),
-    ('K', 0), ('z', 5, 'T0'), ('z', 6, 'T0'), ('J', 2), ('x', 5, 1), ('x', 5, 0), ('z', 3, 'T3'), ('F', 3),
-    ('z', 4, 'T3'), ('H', 1), ('F', 4), ('G', 3), ('z', 5, 'T1'), ('z', 6, 'T1'), ('x', 6, 0), ('J', 1), ('L', 0),
-    ('z', 5, 'T2'), ('z', 6, 'T2'), ('G', 4), ('x', 6, 1), ('K', 2), ('z', 7, 'C'), ('xb', 5), ('z', 7, 'T0'),
-    ('H', 3), ('xb', 6), ('K', 1), ('z', 5, 'T3'), ('z', 6, 'T3'), ('F', 5), ('z', 7, 'T1'), ('M', 0), ('J', 3),
-    ('z', 7, 'T2'), ('G', 5), ('F', 6), ('z', 7, 'T3'), ('x', 7, 1), ('x', 7, 0), ('L', 2), ('H', 4), ('G', 6),
-    ('J', 4), ('L', 1), ('K', 3), ('H', 5), ('xb', 7), ('F', 7), ('J', 5), ('M', 2), ('G', 7), ('K', 4), ('L', 3),
-    ('H', 6), ('M', 1), ('K', 5), ('J', 6), ('L', 4), ('H', 7), ('M', 3), ('L', 5), ('J', 7), ('M', 4), ('K', 6),
-    ('ht',), ('W', 0), ('W', 1), ('W', 2), ('W', 3), ('W', 4), ('L', 7), ('W', 5), ('W', 6), ('L', 6), ('W', 7),
+    ('xb', 1), ('z', 3, 'T0'), ('z', 4, 'T0'), ('xb', 2), ('G', 0), ('z', 1, 'T3'), ('z', 2, 'T3'), ('F', 1),
+    ('x', 3, 0), ('x', 3, 1), ('F', 2), ('z', 3, 'T1'), ('z', 4, 'T1'), ('G', 1), ('x', 4, 0), ('x', 4, 1), ('H', 0),
+    ('G', 2), ('xb', 3), ('z', 3, 'T2'), ('z', 4, 'T2'), ('J', 0), ('z', 5, 'C'), ('z', 6, 'C'), ('t3', 3), ('F', 3),
+    ('xb', 4), ('H', 1), ('t3', 4), ('F', 4), ('z', 5, 'T0'), ('z', 6, 'T0'), ('G', 3), ('J', 1), ('H', 2),
+    ('z', 5, 'T1'), ('z', 6, 'T1'), ('x', 5, 0), ('x', 5, 1), ('G', 4), ('J', 2), ('z', 5, 'T2'), ('z', 6, 'T2'),
+    ('K', 1), ('z', 7, 'C'), ('x', 6, 0), ('x', 6, 1), ('Y', 0), ('z', 7, 'T0'), ('z', 7, 'T1'), ('xb', 5),
+    ('t3', 5), ('F', 5), ('K', 2), ('t3', 6), ('z', 7, 'C1'), ('H', 3), ('G', 5), ('z', 7, 'T2'), ('z', 7, 'C2'),
+    ('J', 3), ('L', 1), ('xb', 6), ('F', 6), ('K', 0), ('H', 4), ('G', 6), ('z', 7, 'C3'), ('J', 4), ('H', 5),
+    ('L', 2), ('M', 1), ('t3', 7), ('K', 3), ('F', 7), ('J', 5), ('K', 4), ('G', 7), ('H', 6), ('L', 0), ('M', 2),
+    ('J', 6), ('L', 3), ('K', 5), ('L', 4), ('H', 7), ('K', 6), ('M', 3), ('J', 7), ('ht',), ('L', 5), ('M', 4),
+    ('W', 0), ('W', 1), ('L', 6), ('M', 5), ('W', 2), ('W', 3), ('W', 4), ('L', 7), ('W', 5), ('W', 6), ('W', 7),
     ('N',),
 )
 
@@ -54,15 +55,14 @@
         (self.tok_in, self.cot_in, self.wg_in, self.wu_in, self.wd_in,
          self.out, self.og, self.ou, self.od,
          self.tok, self.cot, self.wg, self.wu, self.wd, self.part, self.s1, self.g2, self.s2, self.back,
-         self.tot, self.b1, self.b2, self.r1, self.r2, self.by, self.ry, self.bz, self.rz,
-         self.vg, self.vu, self.vd, self.ht, self.send_sem, self.recv_sem, self.local_sem) = refs
+         self.tot, self.b1, self.b2, self.r1, self.r2, self.by, self.ry, self.bz, self.rz, self.by4, self.ry4,
+         self.ht, self.send_sem, self.recv_sem, self.local_sem) = refs
         hid, mod = lax.axis_index("hid"), lax.axis_index("mod")
         self.x, self.yl, self.z = hid // 16, (hid // 8) % 2, hid % 8
         self.yh, self.c = mod // 2, mod % 2
         self.ids = {}
         self.sent = []
         self.n_local = 0
-        self.local = []
         half = self.tok.shape[1] // 2
         self.half = (pl.ds(0, half), pl.ds(half, half))
 
@@ -173,7 +173,8 @@
         if a == "T":
             r = self.tok.at[self.rows(0, 2)]
             for p in (0, 1):
-                self.send(("z", 1 + p, "T3", 0), r, r, self.zd(p))
+                if 1 + p not in TX:
+                    self.send(("z", 1 + p, "T3", 0), r, r, self.zd(p))
 
     def zin(self, k, p):
         d = 0 if k % 2 else 1
@@ -188,7 +189,12 @@
                 self.wait(("z", k, p[0] + "o", part), a.at[self.rows(k, dx, y)], self.zd(1 - d))
         else:
             self.wait(("z", k, p, 0), r, self.zd(1 - d))
-        self.onward(k, p, dx)
+        if p != "T3" or min(k + 2, 7) not in TX:
+            self.onward(k, p, dx)
+        if k in TX and p in ("T1", "T2"):
+            q = 0 if p == "T1" else 1
+            h = a.at[self.rows(k, dx), self.half[q]]
+            self.send(("t3", k, q), h, h, self.xd(q))
         if p == "C" and k not in ZC:
             for q in (0, 1):
                 self.send(("x", k, q), r, r, self.xd(q))
@@ -202,6 +208,12 @@
         elif k < 7:
             h = a.at[self.rows(k, dx), self.half[d]]
             self.send(("z", 7, p, d), h, h, self.zd(d))
+
+    def t3(self, k):
+        for q in (0, 1):
+            self.wait(("t3", k, q), self.tok.at[self.rows(k, 2), self.half[q]], self.xd(1 - q))
+        if min(k + 2, 7) not in TX:
+            self.onward(k, "T3", 2)
 
     def xin(self, k, q):
         dx = -1 if q == 0 else 1
@@ -259,36 +271,64 @@
         self.tot[k] = jnp.dot(self.back[1, r, :], self.wg[...], preferred_element_type=F32) + jnp.dot(
             self.back[2, r, :], self.wu[...], preferred_element_type=F32
         )
-        self.b1[k] = self.tot[k, self.block(2), :].astype(BF)
+        if k in YF:
+            i = YF.index(k)
+            for b in range(NX):
+                self.by4[i, b * SH : (b + 1) * SH] = self.tot[k, self.strip(b, 1 - self.yl), :].astype(BF)
+            self.send(("ry", k), self.by4.at[i], self.ry4.at[i], self.dev(yl=1 - self.yl))
+        else:
+            self.over_x(k)
+
+    def strip(self, b, y):
+        return pl.ds(pl.multiple_of(b * PAIR + y * SH, SH), SH)
+
+    def Y(self, k):
+        i = YF.index(k)
+        self.wait(("ry", k), self.ry4.at[i], self.dev(yl=1 - self.yl))
+        for b in range(NX):
+            r = self.strip(b, self.yl)
+            self.tot[k, r, :] = self.tot[k, r, :] + self.ry4[i, b * SH : (b + 1) * SH].astype(F32)
+        self.over_x(k)
+
+    def block(self, k, dx):
+        if k in YF:
+            return self.strip(self.xblock(dx), self.yl)
+        return pl.ds(pl.multiple_of(self.xblock(dx) * PAIR, PAIR), PAIR)
+
+    def over_x(self, k):
+        n = pl.ds(0, SH if k in YF else PAIR)
+        self.b1[k, n] = self.tot[k, self.block(k, 2), :].astype(BF)
         if k in DIRECT:
-            self.send(("r1", k), self.b1.at[k], self.r1.at[k], self.dev(dx=2))
+            self.send(("r1", k), self.b1.at[k, n], self.r1.at[k, n], self.dev(dx=2))
             for q in (0, 1):
-                self.b2[k, q] = self.tot[k, self.block(1 if q == 0 else -1), :].astype(BF)
-                self.send(("r2", k, q), self.b2.at[k, q], self.r2.at[k, q], self.xd(q))
+                self.b2[k, q, n] = self.tot[k, self.block(k, 1 if q == 0 else -1), :].astype(BF)
+                self.send(("r2", k, q), self.b2.at[k, q, n], self.r2.at[k, q, n], self.xd(q))
         else:
             for q in (0, 1):
-                self.send(("r1", k, q), self.b1.at[k, :, self.half[q]], self.r1.at[k, :, self.half[q]], self.xd(q))
-
-    def block(self, dx):
-        return pl.ds(pl.multiple_of(self.xblock(dx) * PAIR, PAIR), PAIR)
+                self.send(("r1", k, q), self.b1.at[k, n, self.half[q]], self.r1.at[k, n, self.half[q]], self.xd(q))
 
     def K(self, k):
+        n = pl.ds(0, SH if k in YF else PAIR)
         for q in (0, 1):
             h, o = self.half[q], self.half[1 - q]
-            self.wait(("r1", k, q), self.r1.at[k, :, h], self.xd(1 - q))
-            b = self.block(1 if q == 0 else -1)
-            self.b2[k, q, :, h] = (self.tot[k, b, h] + self.r1[k, :, h].astype(F32)).astype(BF)
-            self.b2[k, q, :, o] = self.tot[k, b, o].astype(BF)
-            self.send(("r2", k, q), self.b2.at[k, q], self.r2.at[k, q], self.xd(q))
+            self.wait(("r1", k, q), self.r1.at[k, n, h], self.xd(1 - q))
+            b = self.block(k, 1 if q == 0 else -1)
+            self.b2[k, q, n, h] = (self.tot[k, b, h] + self.r1[k, n, h].astype(F32)).astype(BF)
+            self.b2[k, q, n, o] = self.tot[k, b, o].astype(BF)
+            self.send(("r2", k, q), self.b2.at[k, q, n], self.r2.at[k, q, n], self.xd(q))
 
     def L(self, k):
-        for q in (0, 1):
-            self.wait(("r2", k, q), self.r2.at[k, q], self.xd(1 - q))
-        b = self.block(0)
-        s = self.tot[k, b, :] + self.r2[k, 0].astype(F32) + self.r2[k, 1].astype(F32)
+        n = pl.ds(0, SH if k in YF else PAIR)
+        for q in (0, 1):
+            self.wait(("r2", k, q), self.r2.at[k, q, n], self.xd(1 - q))
+        b = self.block(k, 0)
+        s = self.tot[k, b, :] + self.r2[k, 0, n].astype(F32) + self.r2[k, 1, n].astype(F32)
         if k in DIRECT:
-            self.wait(("r1", k), self.r1.at[k], self.dev(dx=2))
-            s = s + self.r1[k].astype(F32)
+            self.wait(("r1", k), self.r1.at[k, n], self.dev(dx=2))
+            s = s + self.r1[k, n].astype(F32)
+        if k in YF:
+            self.over_z(k, s)
+            return
         self.tot[k, b, :] = s
         if k in FAR:
             for i, y in ((0, self.yl), (1, 1 - self.yl)):
@@ -299,21 +339,23 @@
             self.send(("ry", k), self.by.at[k], self.ry.at[k], self.dev(yl=1 - self.yl))
 
     def yrows(self, y):
-        return pl.ds(pl.multiple_of(self.xblock(0) * PAIR + y * SH, SH), SH)
-
-    def M(self, k):
-        self.wait(("ry", k), self.ry.at[k], self.dev(yl=1 - self.yl))
-        s = self.tot[k, self.yrows(self.yl), :] + self.ry[k].astype(F32)
+        return self.strip(self.xblock(0), y)
+
+    def over_z(self, k, s):
         if k == 0:
             self.tot[k, self.yrows(self.yl), :] = s
         else:
             self.bz[k, 0] = s.astype(BF)
             self.send(("rz", k, 0), self.bz.at[k, 0], self.rz.at[k, 0], self.dev(dz=offset(k)))
 
+    def M(self, k):
+        self.wait(("ry", k), self.ry.at[k], self.dev(yl=1 - self.yl))
+        self.over_z(k, self.tot[k, self.yrows(self.yl), :] + self.ry[k].astype(F32))
+
     def N(self):
         s = self.tot[0, self.yrows(self.yl), :]
         for k in range(1, NZ):
-            for i, y in ((0, self.yl), (1, 1 - self.yl))[: 2 if k in FAR else 1]:
+            for i, y in ((0, self.yl), (1, 1 - self.yl))[: 2 if k in FAR and k not in YF else 1]:
                 self.wait(("rz", k, i), self.rz.at[k, i], self.dev(dz=-offset(k), yl=y))
                 s = s + self.rz[k, i].astype(F32)
         self.out[...] = s.astype(BF)
@@ -325,16 +367,13 @@
     def W(self, j):
         n = self.tok.shape[1] // TILES
         cs = pl.ds(j * n, n)
-        for i, a, v, o in ((1, self.tok, self.vg, self.og), (2, self.tok, self.vu, self.ou), (0, self.cot, self.vd, self.od)):
-            v[:, cs] = jnp.dot(self.ht[i], a[:, cs], preferred_element_type=F32).astype(BF)
-            self.local.append(self.fetch(v.at[:, cs], o.at[:, cs]))
+        for i, a, o in ((1, self.tok, self.og), (2, self.tok, self.ou), (0, self.cot, self.od)):
+            o[:, cs] = jnp.dot(self.ht[i], a[:, cs], preferred_element_type=F32).astype(BF)
 
     def finish(self):
         self.ready()
         for cp in self.sent:
             cp.wait_send()
-        for cp in self.local:
-            cp.wait()
 
 
 NAMES = {"z": "zin", "x": "xin", "ht": "turn"}
@@ -348,26 +387,21 @@
     step.finish()
 
 
-def hand_over(*refs):
-    for src, dst in zip(refs[:4], refs[4:]):
-        dst[...] = src[...]
-
-
 def shards(tokens, grad_output, gate_weight, up_weight, down_weight):
     d, f = gate_weight.shape
     n = NZ * CHUNK
     anywhere = pl.BlockSpec(memory_space=pl.ANY)
     vmem = pltpu.VMEM
-    results = pl.pallas_call(
+    grad_tokens, grad_gate, grad_up, grad_down = pl.pallas_call(
         kernel,
         out_shape=(
             jax.ShapeDtypeStruct((SH, d), BF),
-            jax.ShapeDtypeStruct((f, d), BF),
-            jax.ShapeDtypeStruct((f, d), BF),
-            jax.ShapeDtypeStruct((f, d), BF),
+            vmem((f, d), BF),
+            vmem((f, d), BF),
+            vmem((f, d), BF),
         ),
         in_specs=[anywhere] * 5,
-        out_specs=(pl.BlockSpec(memory_space=vmem), anywhere, anywhere, anywhere),
+        out_specs=(pl.BlockSpec(memory_space=vmem),) * 4,
         scratch_shapes=[
             vmem((n, d), BF), vmem((n, d), BF),
             vmem((f, d), BF), vmem((f, d), BF), vmem((f, d), BF),
@@ -377,20 +411,13 @@
             vmem((NZ, PAIR, d), BF), vmem((NZ, 2, PAIR, d), BF),
             vmem((NZ, PAIR, d), BF), vmem((NZ, 2, PAIR, d), BF),
             vmem((NZ, SH, d), BF), vmem((NZ, SH, d), BF), vmem((NZ, 2, SH, d), BF), vmem((NZ, 2, SH, d), BF),
-            vmem((f, d), BF), vmem((f, d), BF), vmem((f, d), BF), vmem((3, f, n), BF),
-            pltpu.SemaphoreType.DMA((200,)), pltpu.SemaphoreType.DMA((200,)), pltpu.SemaphoreType.DMA((5 + 3 * TILES,)),
+            vmem((max(1, len(YF)), NX * SH, d), BF), vmem((max(1, len(YF)), NX * SH, d), BF),
+            vmem((3, f, n), BF),
+            pltpu.SemaphoreType.DMA((200,)), pltpu.SemaphoreType.DMA((200,)), pltpu.SemaphoreType.DMA((5,)),
         ],
-        compiler_params=pltpu.CompilerParams(collective_id=0, has_side_effects=True, vmem_limit_bytes=62 << 20),
+        compiler_params=pltpu.CompilerParams(collective_id=0, has_side_effects=True, vmem_limit_bytes=57 << 20),
         cost_estimate=pl.CostEstimate(flops=16 * n * d * f, bytes_accessed=12 * d * f, transcendentals=n * f),
     )(tokens, grad_output, gate_weight.T, up_weight.T, down_weight)
-    blocks = [pl.BlockSpec((SH, d), lambda i: (0, 0))] + [pl.BlockSpec((f // COPIES, d), lambda i: (i, 0))] * 3
-    grad_tokens, grad_gate, grad_up, grad_down = pl.pallas_call(
-        hand_over,
-        grid=(COPIES,),
-        out_shape=tuple(jax.ShapeDtypeStruct(r.shape, r.dtype) for r in results),
-        in_specs=blocks,
-        out_specs=tuple(blocks),
-    )(*results)
     return grad_tokens, grad_gate.T, grad_up.T, grad_down
 
 

time: 121 us -> 115 us (0.950)
  Pallas kernels: 120 us -> 110 us
  local copies, waits for them, and re-layouts: 0 us -> 4.32 us
    pallas_call x2 -> x1, Pallas kernels: 120 us -> 110 us  [shards(): pl.pallas_call(kernel, out_shape=(jax.ShapeDtypeStruct((SH, d), BF), vmem...]
    unnamed x0 -> x6, local copies, waits for them, and re-layouts: none -> 4.32 us
where the time goes in v3:
time: 115 us
  Pallas kernels  110 us (96%)
  local copies, waits for them, and re-layouts  4.32 us (4%)
    pallas_call x1, Pallas kernels, shards(): pl.pallas_call(kernel, out_shape=(jax.ShapeDtypeStruct((SH, d), BF), vmem...  110 us
    unnamed x6, local copies, waits for them, and re-layouts  4.32 us

profile of v3, /device:TPU:1, one launch (start us, length us, event | category | flops | bytes accessed | tf_op | source)
XLA Modules:
  0.0 114.5 jit_solution(8181809107577098715)
XLA Ops:
  0.6 109.6 %shard_map.84 = (bf16[16,2048]{1,0:T(8,128)(2,1)}, bf16[448,2048]{1,0:T(8,128)(2,1)S(1)}, bf16[448,2048]{1,0:T(8,128)(2,1)S(1)}, bf16[448,2048]{1,0:T(8,128)(2,1)S(1)}) custom-call(bf16[16,2048]{1,0:T(8,128)(2,1)} %refs_0_.1, bf16[16,2048]{1,0:T(8,128)(2,1)} %refs_1_.1, bf16[448,2048]{1,0:T(8,128)(2,1)} %bitcast.6, bf16[448,2048]{1,0:T(8,128)(2,1)} %bitcast.7, ...), custom_call_target="tpu_custom_call" | custom-call | flops 15032385536 | bytes 11010048 | tf_op jit(solution)/shard_map/pallas_call | solution.py:395
  110.2 1.2 %copy.13 = bf16[2048,448]{0,1:T(8,128)(2,1)} copy(bf16[2048,448]{0,1:T(8,128)(2,1)S(1)} %bitcast.5) | data formatting | bytes 3670016
  111.5 1.2 %copy.14 = bf16[2048,448]{0,1:T(8,128)(2,1)} copy(bf16[2048,448]{0,1:T(8,128)(2,1)S(1)} %bitcast.4) | data formatting | bytes 3670016
  112.7 0.0 copy-start
  112.7 1.2 %copy.15 = bf16[448,2048]{1,0:T(8,128)(2,1)} copy(bf16[448,2048]{1,0:T(8,128)(2,1)S(1)} %get-tuple-element.15) | data formatting | bytes 3670016
  113.9 0.0 copy-done
  113.9 0.6 copy.16
Async XLA Ops:
  112.7 1.2 %copy-start = (bf16[16,2048]{1,0:T(8,128)(2,1)S(1)}, bf16[16,2048]{1,0:T(8,128)(2,1)}, u32[]{:S(2)}) copy-start(bf16[16,2048]{1,0:T(8,128)(2,1)} %get-tuple-element.20) | copy-start | bytes 196612

commit v4 on v3

--- a/solution.py
+++ b/solution.py
@@ -18,27 +18,29 @@
 CHUNK = NX * PAIR
 TILES = 8
 ZC = (7,)
-TX = (3, 4, 5, 6, 7)
-YF = (0,)
-DIRECT = (7,)
-FAR = (6, 7)
+TX = (1, 2, 3, 6)
+YC = (0, 1, 4)
+YF = (2, 6)
+DIRECT = (2, 6, 7)
+FAR = (5,)
 
 ORDER = (
-    ('own',), ('y',), ('x0', 'T', 0), ('x0', 'T', 1), ('z', 1, 'C'), ('z', 2, 'C'), ('z', 1, 'T0'), ('z', 2, 'T0'),
-    ('x0', 'C', 0), ('x0', 'C', 1), ('x0b', 'T'), ('z', 1, 'T1'), ('z', 2, 'T1'), ('x', 1, 0), ('x', 1, 1),
-    ('z', 1, 'T2'), ('z', 2, 'T2'), ('x', 2, 0), ('x', 2, 1), ('z', 3, 'C'), ('z', 4, 'C'), ('x0b', 'C'), ('F', 0),
-    ('xb', 1), ('z', 3, 'T0'), ('z', 4, 'T0'), ('xb', 2), ('G', 0), ('z', 1, 'T3'), ('z', 2, 'T3'), ('F', 1),
-    ('x', 3, 0), ('x', 3, 1), ('F', 2), ('z', 3, 'T1'), ('z', 4, 'T1'), ('G', 1), ('x', 4, 0), ('x', 4, 1), ('H', 0),
-    ('G', 2), ('xb', 3), ('z', 3, 'T2'), ('z', 4, 'T2'), ('J', 0), ('z', 5, 'C'), ('z', 6, 'C'), ('t3', 3), ('F', 3),
-    ('xb', 4), ('H', 1), ('t3', 4), ('F', 4), ('z', 5, 'T0'), ('z', 6, 'T0'), ('G', 3), ('J', 1), ('H', 2),
-    ('z', 5, 'T1'), ('z', 6, 'T1'), ('x', 5, 0), ('x', 5, 1), ('G', 4), ('J', 2), ('z', 5, 'T2'), ('z', 6, 'T2'),
-    ('K', 1), ('z', 7, 'C'), ('x', 6, 0), ('x', 6, 1), ('Y', 0), ('z', 7, 'T0'), ('z', 7, 'T1'), ('xb', 5),
-    ('t3', 5), ('F', 5), ('K', 2), ('t3', 6), ('z', 7, 'C1'), ('H', 3), ('G', 5), ('z', 7, 'T2'), ('z', 7, 'C2'),
-    ('J', 3), ('L', 1), ('xb', 6), ('F', 6), ('K', 0), ('H', 4), ('G', 6), ('z', 7, 'C3'), ('J', 4), ('H', 5),
-    ('L', 2), ('M', 1), ('t3', 7), ('K', 3), ('F', 7), ('J', 5), ('K', 4), ('G', 7), ('H', 6), ('L', 0), ('M', 2),
-    ('J', 6), ('L', 3), ('K', 5), ('L', 4), ('H', 7), ('K', 6), ('M', 3), ('J', 7), ('ht',), ('L', 5), ('M', 4),
-    ('W', 0), ('W', 1), ('L', 6), ('M', 5), ('W', 2), ('W', 3), ('W', 4), ('L', 7), ('W', 5), ('W', 6), ('W', 7),
-    ('N',),
+    ('own',), ('y',), ('x0', 'C', 0), ('x0', 'C', 1), ('x0', 'T', 0), ('x0', 'T', 1), ('z', 1, 'C'), ('z', 2, 'C'),
+    ('cx', 2), ('x0b', 'C'), ('cx', 1), ('z', 1, 'T0'), ('z', 2, 'T0'), ('x0b', 'T'), ('yc', 0), ('F', 0),
+    ('z', 1, 'T1'), ('z', 2, 'T1'), ('x', 2, 0), ('x', 2, 1), ('G', 0), ('z', 1, 'T2'), ('x', 1, 0), ('x', 1, 1),
+    ('z', 2, 'T2'), ('z', 3, 'C'), ('z', 4, 'C'), ('cx', 4), ('cx', 3), ('t3', 1), ('xb', 2), ('xb', 1),
+    ('z', 3, 'T0'), ('z', 4, 'T0'), ('t3', 2), ('H', 0), ('x', 4, 0), ('F', 2), ('x', 4, 1), ('J', 0),
+    ('z', 3, 'T1'), ('z', 4, 'T1'), ('yc', 1), ('G', 2), ('x', 3, 0), ('x', 3, 1), ('F', 1), ('z', 3, 'T2'),
+    ('z', 4, 'T2'), ('xb', 4), ('K', 0), ('G', 1), ('z', 5, 'C'), ('z', 6, 'C'), ('cx', 5), ('cx', 6), ('t3', 3),
+    ('xb', 3), ('F', 3), ('z', 5, 'T0'), ('z', 6, 'T0'), ('H', 2), ('yc', 4), ('L', 0), ('G', 3), ('J', 2),
+    ('z', 4, 'T3'), ('F', 4), ('z', 5, 'T1'), ('z', 5, 'T2'), ('z', 6, 'T1'), ('x', 5, 0), ('x', 5, 1), ('H', 1),
+    ('M', 0), ('G', 4), ('x', 6, 0), ('x', 6, 1), ('J', 1), ('z', 6, 'T2'), ('H', 3), ('z', 5, 'T3'), ('z', 7, 'C'),
+    ('xb', 5), ('F', 5), ('z', 7, 'T0'), ('xb', 6), ('J', 3), ('z', 7, 'T1'), ('K', 1), ('t3', 6), ('F', 6),
+    ('z', 7, 'C1'), ('Y', 2), ('G', 5), ('z', 7, 'T2'), ('z', 7, 'C2'), ('K', 3), ('G', 6), ('H', 4), ('z', 7, 'T3'),
+    ('z', 7, 'C3'), ('F', 7), ('J', 4), ('G', 7), ('H', 5), ('L', 1), ('L', 2), ('J', 5), ('L', 3), ('H', 6),
+    ('K', 4), ('J', 6), ('K', 5), ('H', 7), ('M', 1), ('J', 7), ('M', 3), ('ht',), ('L', 4), ('W', 0), ('L', 5),
+    ('W', 1), ('W', 2), ('Y', 6), ('W', 3), ('L', 7), ('M', 4), ('W', 4), ('W', 5), ('L', 6), ('M', 7), ('W', 6),
+    ('W', 7), ('N',),
 )
 
 
@@ -154,27 +156,37 @@
         for a in "TC":
             self.wait(("y", a), self.arr(a).at[self.rows(0, 0, 1 - self.yl)], self.dev(yl=1 - self.yl))
         for to, a in (("x", "T"), ("x", "C"), ("z", "C"), ("z", "T")):
-            self.plane(to, a, 1 - self.yl, 1)
+            if (to, a) != ("x", "C") or 0 not in YC:
+                self.plane(to, a, 1 - self.yl, 1)
 
     def x0(self, a, q):
         dx = -1 if q == 0 else 1
-        for part, y in ((0, self.yl), (1, 1 - self.yl)):
+        ys = (self.yl, 1 - self.yl)
+        if a == "C" and 0 in YC:
+            ys = ys[:1]
+        for part, y in enumerate(ys):
             self.wait(("x0", a, q, part), self.arr(a).at[self.rows(0, dx, y)], self.xd(1 - q))
-        r = self.arr(a).at[self.rows(0, dx)]
-        h = self.arr(a).at[self.rows(0, dx), self.half[q]]
+        rows = self.crows(0, dx) if a == "C" else self.rows(0, dx)
+        r = self.arr(a).at[rows]
+        h = self.arr(a).at[rows, self.half[q]]
         self.send(("x0b", a, q), h, h, self.xd(q))
         if a == "T":
             for p in (0, 1):
                 self.send(("z", 1 + p, "T%d" % (1 + q), 0), r, r, self.zd(p))
+        else:
+            self.gathered(0, q, dx, r)
 
     def x0b(self, a):
-        for q in (0, 1):
-            self.wait(("x0b", a, q), self.arr(a).at[self.rows(0, 2), self.half[q]], self.xd(1 - q))
+        rows = self.crows(0, 2) if a == "C" else self.rows(0, 2)
+        for q in (0, 1):
+            self.wait(("x0b", a, q), self.arr(a).at[rows, self.half[q]], self.xd(1 - q))
+        r = self.arr(a).at[rows]
         if a == "T":
-            r = self.tok.at[self.rows(0, 2)]
             for p in (0, 1):
                 if 1 + p not in TX:
                     self.send(("z", 1 + p, "T3", 0), r, r, self.zd(p))
+        else:
+            self.gathered(0, 2, 2, r)
 
     def zin(self, k, p):
         d = 0 if k % 2 else 1
@@ -195,9 +207,6 @@
             q = 0 if p == "T1" else 1
             h = a.at[self.rows(k, dx), self.half[q]]
             self.send(("t3", k, q), h, h, self.xd(q))
-        if p == "C" and k not in ZC:
-            for q in (0, 1):
-                self.send(("x", k, q), r, r, self.xd(q))
 
     def onward(self, k, p, dx):
         d = 0 if k % 2 else 1
@@ -215,19 +224,39 @@
         if min(k + 2, 7) not in TX:
             self.onward(k, "T3", 2)
 
+    def crows(self, k, dx):
+        return self.rows(k, dx, self.yl if k in YC else None)
+
+    def cx(self, k):
+        r = self.cot.at[self.crows(k, 0)]
+        for q in (0, 1):
+            self.send(("x", k, q), r, r, self.xd(q))
+
     def xin(self, k, q):
         dx = -1 if q == 0 else 1
-        self.wait(("x", k, q), self.cot.at[self.rows(k, dx)], self.xd(1 - q))
-        h = self.cot.at[self.rows(k, dx), self.half[q]]
+        r = self.cot.at[self.crows(k, dx)]
+        self.wait(("x", k, q), r, self.xd(1 - q))
+        h = self.cot.at[self.crows(k, dx), self.half[q]]
         self.send(("xb", k, q), h, h, self.xd(q))
-        if min(k + 2, 7) in ZC:
-            self.onward(k, "C%d" % (1 + q), dx)
+        self.gathered(k, q, dx, r)
 
     def xb(self, k):
         for q in (0, 1):
-            self.wait(("xb", k, q), self.cot.at[self.rows(k, 2), self.half[q]], self.xd(1 - q))
-        if min(k + 2, 7) in ZC:
-            self.onward(k, "C3", 2)
+            self.wait(("xb", k, q), self.cot.at[self.crows(k, 2), self.half[q]], self.xd(1 - q))
+        self.gathered(k, 2, 2, self.cot.at[self.crows(k, 2)])
+
+    def gathered(self, k, i, dx, r):
+        if k in YC:
+            self.send(("yc", k, i), r, r, self.dev(yl=1 - self.yl))
+        elif k and min(k + 2, 7) in ZC:
+            self.onward(k, "C%d" % (1 + i), dx)
+
+    def yc(self, k):
+        for i, dx in enumerate((-1, 1, 2)):
+            self.wait(("yc", k, i), self.cot.at[self.rows(k, dx, 1 - self.yl)], self.dev(yl=1 - self.yl))
+        if k and min(k + 2, 7) in ZC:
+            for i, dx in enumerate((-1, 1, 2)):
+                self.onward(k, "C%d" % (1 + i), dx)
 
     def ready(self):
         for cp in self.weights:
@@ -247,21 +276,32 @@
     def G(self, k):
         self.wait(("s1", k), self.s1.at[k], self.dev(c=1 - self.c))
         mine = pl.ds(pl.multiple_of(self.c * 64, 64), 64)
+        rest = []
         for i in range(3):
             total = self.part[k, i, mine, :] + self.s1[k, i]
             self.s1[k, i] = total
-            self.g2[k, i] = total.astype(BF)
+            low = total.astype(BF)
+            for t in range(3):
+                self.g2[k, (i * 3 + t) * 64 : (i * 3 + t + 1) * 64, :] = low[:, t * 128 : (t + 1) * 128]
+            rest.append(low[:, 384:])
+        self.g2[k, 576:640, :] = jnp.concatenate(rest[:2], axis=1)
+        self.g2[k, 640:, :] = jnp.concatenate([rest[2][:32], rest[2][32:]], axis=1)
         self.send(("s2", k), self.g2.at[k], self.s2.at[k], self.dev(yh=1 - self.yh))
 
     def H(self, k):
         self.wait(("s2", k), self.s2.at[k], self.dev(yh=1 - self.yh))
-        gate, up, grad = (self.s1[k, i] + self.s2[k, i].astype(F32) for i in range(3))
-        s = jax.nn.sigmoid(gate)
-        a = gate * s
         r = self.side(k, self.c)
-        self.back[0, r, :] = (a * up).astype(BF)
-        self.back[1, r, :] = (grad * up * (s * (1.0 + gate * (1.0 - s)))).astype(BF)
-        self.back[2, r, :] = (grad * a).astype(BF)
+        pair, last = self.s2[k, 576:640, :], self.s2[k, 640:, :]
+        rest = (pair[:, :64], pair[:, 64:], jnp.concatenate([last[:, :64], last[:, 64:]], axis=0))
+        for t in range(4):
+            cs = pl.ds(t * 128, 128 if t < 3 else 64)
+            far = [self.s2[k, (i * 3 + t) * 64 : (i * 3 + t + 1) * 64, :] if t < 3 else rest[i] for i in range(3)]
+            gate, up, grad = (self.s1[k, i, :, cs] + far[i].astype(F32) for i in range(3))
+            s = jax.nn.sigmoid(gate)
+            a = gate * s
+            self.back[0, r, cs] = (a * up).astype(BF)
+            self.back[1, r, cs] = (grad * up * (s * (1.0 + gate * (1.0 - s)))).astype(BF)
+            self.back[2, r, cs] = (grad * a).astype(BF)
         b = self.back.at[:, r, :]
         self.send(("s4", k), b, b, self.dev(c=1 - self.c))
 
@@ -395,7 +435,7 @@
     grad_tokens, grad_gate, grad_up, grad_down = pl.pallas_call(
         kernel,
         out_shape=(
-            jax.ShapeDtypeStruct((SH, d), BF),
+            vmem((SH, d), BF),
             vmem((f, d), BF),
             vmem((f, d), BF),
             vmem((f, d), BF),
@@ -405,7 +445,7 @@
         scratch_shapes=[
             vmem((n, d), BF), vmem((n, d), BF),
             vmem((f, d), BF), vmem((f, d), BF), vmem((f, d), BF),
-            vmem((NZ, 3, CHUNK, f), F32), vmem((NZ, 3, 64, f), F32), vmem((NZ, 3, 64, f), BF), vmem((NZ, 3, 64, f), BF),
+            vmem((NZ, 3, CHUNK, f), F32), vmem((NZ, 3, 64, f), F32), vmem((NZ, 672, 128), BF), vmem((NZ, 672, 128), BF),
             vmem((3, n, f), BF),
             vmem((NZ, CHUNK, d), F32),
             vmem((NZ, PAIR, d), BF), vmem((NZ, 2, PAIR, d), BF),

time: 115 us -> 107 us (0.930)
  Pallas kernels: 110 us -> 102 us
    pallas_call x1, Pallas kernels: 110 us -> 102 us  [shards(): pl.pallas_call(kernel, out_shape=(vmem((SH, d), BF), vmem((f, d), BF), vm...]
    unnamed x6 -> x4, local copies, waits for them, and re-layouts: 4.32 us -> 4.32 us
where the time goes in v4:
time: 107 us
  Pallas kernels  102 us (95%)
  local copies, waits for them, and re-layouts  4.32 us (4%)
    pallas_call x1, Pallas kernels, shards(): pl.pallas_call(kernel, out_shape=(vmem((SH, d), BF), vmem((f, d), BF), vm...  102 us
    unnamed x4, local copies, waits for them, and re-layouts  4.32 us

profile of v4, /device:TPU:1, one launch (start us, length us, event | category | flops | bytes accessed | tf_op | source)
XLA Modules:
  0.0 106.7 jit_solution(18366151454756258358)
XLA Ops:
  0.6 101.8 %shard_map.84 = (bf16[16,2048]{1,0:T(8,128)(2,1)S(1)}, bf16[448,2048]{1,0:T(8,128)(2,1)S(1)}, bf16[448,2048]{1,0:T(8,128)(2,1)S(1)}, bf16[448,2048]{1,0:T(8,128)(2,1)S(1)}) custom-call(bf16[16,2048]{1,0:T(8,128)(2,1)} %refs_0_.1, bf16[16,2048]{1,0:T(8,128)(2,1)} %refs_1_.1, bf16[448,2048]{1,0:T(8,128)(2,1)} %bitcast.6, bf16[448,2048]{1,0:T(8,128)(2,1)} %bitcast.7, ...), custom_call_target="tpu_custom_call" | custom-call | flops 15032385536 | bytes 11010048 | tf_op jit(solution)/shard_map/pallas_call | solution.py:435
  102.4 0.6 copy.13
  103.0 1.2 %copy.14 = bf16[2048,448]{0,1:T(8,128)(2,1)} copy(bf16[2048,448]{0,1:T(8,128)(2,1)S(1)} %bitcast.5) | data formatting | bytes 3670016
  104.3 1.2 %copy.15 = bf16[2048,448]{0,1:T(8,128)(2,1)} copy(bf16[2048,448]{0,1:T(8,128)(2,1)S(1)} %bitcast.4) | data formatting | bytes 3670016
  105.5 1.2 %copy.16 = bf16[448,2048]{1,0:T(8,128)(2,1)} copy(bf16[448,2048]{1,0:T(8,128)(2,1)S(1)} %get-tuple-element.15) | data formatting | bytes 3670016

commit v5 on v4

--- a/solution.py
+++ b/solution.py
@@ -19,28 +19,28 @@
 TILES = 8
 ZC = (7,)
 TX = (1, 2, 3, 6)
-YC = (0, 1, 4)
+YC = (1, 7)
 YF = (2, 6)
-DIRECT = (2, 6, 7)
-FAR = (5,)
+DIRECT = (6, 7)
+FAR = (5, 6)
 
 ORDER = (
-    ('own',), ('y',), ('x0', 'C', 0), ('x0', 'C', 1), ('x0', 'T', 0), ('x0', 'T', 1), ('z', 1, 'C'), ('z', 2, 'C'),
-    ('cx', 2), ('x0b', 'C'), ('cx', 1), ('z', 1, 'T0'), ('z', 2, 'T0'), ('x0b', 'T'), ('yc', 0), ('F', 0),
-    ('z', 1, 'T1'), ('z', 2, 'T1'), ('x', 2, 0), ('x', 2, 1), ('G', 0), ('z', 1, 'T2'), ('x', 1, 0), ('x', 1, 1),
-    ('z', 2, 'T2'), ('z', 3, 'C'), ('z', 4, 'C'), ('cx', 4), ('cx', 3), ('t3', 1), ('xb', 2), ('xb', 1),
-    ('z', 3, 'T0'), ('z', 4, 'T0'), ('t3', 2), ('H', 0), ('x', 4, 0), ('F', 2), ('x', 4, 1), ('J', 0),
-    ('z', 3, 'T1'), ('z', 4, 'T1'), ('yc', 1), ('G', 2), ('x', 3, 0), ('x', 3, 1), ('F', 1), ('z', 3, 'T2'),
-    ('z', 4, 'T2'), ('xb', 4), ('K', 0), ('G', 1), ('z', 5, 'C'), ('z', 6, 'C'), ('cx', 5), ('cx', 6), ('t3', 3),
-    ('xb', 3), ('F', 3), ('z', 5, 'T0'), ('z', 6, 'T0'), ('H', 2), ('yc', 4), ('L', 0), ('G', 3), ('J', 2),
-    ('z', 4, 'T3'), ('F', 4), ('z', 5, 'T1'), ('z', 5, 'T2'), ('z', 6, 'T1'), ('x', 5, 0), ('x', 5, 1), ('H', 1),
-    ('M', 0), ('G', 4), ('x', 6, 0), ('x', 6, 1), ('J', 1), ('z', 6, 'T2'), ('H', 3), ('z', 5, 'T3'), ('z', 7, 'C'),
-    ('xb', 5), ('F', 5), ('z', 7, 'T0'), ('xb', 6), ('J', 3), ('z', 7, 'T1'), ('K', 1), ('t3', 6), ('F', 6),
-    ('z', 7, 'C1'), ('Y', 2), ('G', 5), ('z', 7, 'T2'), ('z', 7, 'C2'), ('K', 3), ('G', 6), ('H', 4), ('z', 7, 'T3'),
-    ('z', 7, 'C3'), ('F', 7), ('J', 4), ('G', 7), ('H', 5), ('L', 1), ('L', 2), ('J', 5), ('L', 3), ('H', 6),
-    ('K', 4), ('J', 6), ('K', 5), ('H', 7), ('M', 1), ('J', 7), ('M', 3), ('ht',), ('L', 4), ('W', 0), ('L', 5),
-    ('W', 1), ('W', 2), ('Y', 6), ('W', 3), ('L', 7), ('M', 4), ('W', 4), ('W', 5), ('L', 6), ('M', 7), ('W', 6),
-    ('W', 7), ('N',),
+    ('own',), ('y',), ('x0', 'T', 0), ('x0', 'T', 1), ('z', 1, 'C'), ('z', 2, 'C'), ('cx', 2), ('cx', 1),
+    ('x0', 'C', 0), ('x0', 'C', 1), ('z', 1, 'T0'), ('z', 2, 'T0'), ('x0b', 'T'), ('A', 0), ('z', 1, 'T1'),
+    ('z', 2, 'T1'), ('x', 2, 0), ('x', 2, 1), ('z', 1, 'T2'), ('z', 2, 'T2'), ('x', 1, 0), ('x', 1, 1), ('x0b', 'C'),
+    ('F', 0), ('z', 3, 'C'), ('z', 4, 'C'), ('cx', 3), ('cx', 4), ('G', 0), ('t3', 1), ('A', 1), ('z', 3, 'T0'),
+    ('z', 4, 'T0'), ('xb', 2), ('t3', 2), ('A', 2), ('F', 2), ('xb', 1), ('z', 3, 'T1'), ('z', 4, 'T1'), ('G', 2),
+    ('x', 3, 0), ('x', 3, 1), ('H', 0), ('yc', 1), ('z', 3, 'T2'), ('z', 4, 'T2'), ('F', 1), ('J', 0), ('G', 1),
+    ('z', 5, 'C'), ('z', 6, 'C'), ('cx', 5), ('x', 4, 0), ('x', 4, 1), ('xb', 3), ('cx', 6), ('t3', 3), ('A', 3),
+    ('F', 3), ('H', 2), ('z', 5, 'T0'), ('z', 6, 'T0'), ('K', 0), ('G', 3), ('J', 2), ('z', 4, 'T3'), ('z', 5, 'T1'),
+    ('A', 4), ('H', 1), ('x', 5, 0), ('x', 5, 1), ('xb', 4), ('F', 4), ('z', 5, 'T2'), ('z', 6, 'T1'), ('J', 1),
+    ('H', 3), ('z', 6, 'T2'), ('x', 6, 0), ('x', 6, 1), ('G', 4), ('J', 3), ('z', 5, 'T3'), ('z', 7, 'C'),
+    ('z', 7, 'T0'), ('xb', 5), ('A', 5), ('F', 5), ('z', 7, 'T1'), ('Y', 2), ('L', 0), ('K', 1), ('t3', 6), ('G', 5),
+    ('A', 6), ('z', 7, 'C1'), ('xb', 6), ('F', 6), ('H', 4), ('z', 7, 'T2'), ('z', 7, 'C2'), ('K', 3), ('K', 2),
+    ('G', 6), ('z', 7, 'T3'), ('A', 7), ('M', 0), ('z', 7, 'C3'), ('F', 7), ('J', 4), ('H', 5), ('G', 7), ('L', 1),
+    ('L', 3), ('J', 5), ('L', 2), ('H', 6), ('K', 4), ('J', 6), ('K', 5), ('H', 7), ('M', 1), ('J', 7), ('M', 3),
+    ('L', 4), ('ht',), ('W', 0), ('L', 5), ('W', 1), ('W', 2), ('Y', 6), ('W', 3), ('L', 7), ('M', 4), ('W', 4),
+    ('W', 5), ('L', 6), ('M', 7), ('W', 6), ('W', 7), ('N',),
 )
 
 
@@ -263,12 +263,15 @@
             cp.wait()
         self.weights = ()
 
-    def F(self, k):
+    def A(self, k):
         self.ready()
         r = self.rows(k)
         t = self.tok[r, :]
         self.part[k, 0] = lax.dot_general(t, self.wg[...], NT, preferred_element_type=F32)
         self.part[k, 1] = lax.dot_general(t, self.wu[...], NT, preferred_element_type=F32)
+
+    def F(self, k):
+        r = self.rows(k)
         self.part[k, 2] = lax.dot_general(self.cot[r, :], self.wd[...], NT, preferred_element_type=F32)
         other = pl.ds(pl.multiple_of((1 - self.c) * 64, 64), 64)
         self.send(("s1", k), self.part.at[k, :, other, :], self.s1.at[k], self.dev(c=1 - self.c))
@@ -427,12 +430,21 @@
     step.finish()
 
 
+def hand_over(*refs):
+    *arrays, sem = refs
+    copies = [pltpu.make_async_copy(arrays[i], arrays[4 + i], sem.at[i]) for i in range(4)]
+    for cp in copies:
+        cp.start()
+    for cp in copies:
+        cp.wait()
+
+
 def shards(tokens, grad_output, gate_weight, up_weight, down_weight):
     d, f = gate_weight.shape
     n = NZ * CHUNK
     anywhere = pl.BlockSpec(memory_space=pl.ANY)
     vmem = pltpu.VMEM
-    grad_tokens, grad_gate, grad_up, grad_down = pl.pallas_call(
+    results = pl.pallas_call(
         kernel,
         out_shape=(
             vmem((SH, d), BF),
@@ -455,9 +467,17 @@
             vmem((3, f, n), BF),
             pltpu.SemaphoreType.DMA((200,)), pltpu.SemaphoreType.DMA((200,)), pltpu.SemaphoreType.DMA((5,)),
         ],
-        compiler_params=pltpu.CompilerParams(collective_id=0, has_side_effects=True, vmem_limit_bytes=57 << 20),
+        compiler_params=pltpu.CompilerParams(collective_id=0, has_side_effects=True, vmem_limit_bytes=55 << 20),
         cost_estimate=pl.CostEstimate(flops=16 * n * d * f, bytes_accessed=12 * d * f, transcendentals=n * f),
     )(tokens, grad_output, gate_weight.T, up_weight.T, down_weight)
+    grad_tokens, grad_gate, grad_up, grad_down = pl.pallas_call(
+        hand_over,
+        out_shape=tuple(jax.ShapeDtypeStruct(r.shape, r.dtype) for r in results),
+        in_specs=[pl.BlockSpec(memory_space=vmem)] * 4,
+        out_specs=(anywhere,) * 4,
+        scratch_shapes=[pltpu.SemaphoreType.DMA((4,))],
+        compiler_params=pltpu.CompilerParams(vmem_limit_bytes=1 << 20),
+    )(*(pltpu.with_memory_space_constraint(r, vmem) for r in results))
     return grad_tokens, grad_gate.T, grad_up.T, grad_down
 
 

time: 107 us -> 105 us (0.981)
  local copies, waits for them, and re-layouts: 4.32 us -> 0 us
  Pallas kernels: 102 us -> 104 us
    unnamed x4 -> x0, local copies, waits for them, and re-layouts: 4.32 us -> none
    pallas_call x0 -> x1, Pallas kernels: none -> 2.49 us  [shards(): pl.pallas_call(hand_over, out_shape=tuple((jax.ShapeDtypeStruct(r.shape,...]
where the time goes in v5:
time: 105 us
  Pallas kernels  104 us (99%)
    pallas_call x1, Pallas kernels, shards(): pl.pallas_call(kernel, out_shape=(vmem((SH, d), BF), vmem((f, d), BF), vm...  102 us
    pallas_call x1, Pallas kernels, shards(): pl.pallas_call(hand_over, out_shape=tuple((jax.ShapeDtypeStruct(r.shape,...  2.49 us

profile of v5, /device:TPU:1, one launch (start us, length us, event | category | flops | bytes accessed | tf_op | source)
XLA Modules:
  0.0 105.0 jit_solution(1879029371604221777)
XLA Ops:
  0.6 101.7 %shard_map.84 = (bf16[16,2048]{1,0:T(8,128)(2,1)S(1)}, bf16[448,2048]{1,0:T(8,128)(2,1)S(1)}, bf16[448,2048]{1,0:T(8,128)(2,1)S(1)}, bf16[448,2048]{1,0:T(8,128)(2,1)S(1)}) custom-call(bf16[16,2048]{1,0:T(8,128)(2,1)} %refs_0_.1, bf16[16,2048]{1,0:T(8,128)(2,1)} %refs_1_.1, bf16[448,2048]{1,0:T(8,128)(2,1)} %bitcast.4, bf16[448,2048]{1,0:T(8,128)(2,1)} %bitcast.5, ...), custom_call_target="tpu_custom_call" | custom-call | flops 15032385536 | bytes 11010048 | tf_op jit(solution)/shard_map/pallas_call | solution.py:447
  102.3 2.5 %shard_map.85 = (bf16[16,2048]{1,0:T(8,128)(2,1)}, bf16[448,2048]{1,0:T(8,128)(2,1)}, bf16[448,2048]{1,0:T(8,128)(2,1)}, bf16[448,2048]{1,0:T(8,128)(2,1)}) custom-call(bf16[16,2048]{1,0:T(8,128)(2,1)S(1)} %get-tuple-element.12.refs_0_, bf16[448,2048]{1,0:T(8,128)(2,1)S(1)} %get-tuple-element.13.refs_1_, bf16[448,2048]{1,0:T(8,128)(2,1)S(1)} %get-tuple-element.14.refs_2_, ...), custom_call_target="tpu_custom_call" | custom-call | tf_op jit(solution)/shard_map/pallas_call | solution.py:473

commit v6 on v5

--- a/solution.py
+++ b/solution.py
@@ -269,15 +269,20 @@
         t = self.tok[r, :]
         self.part[k, 0] = lax.dot_general(t, self.wg[...], NT, preferred_element_type=F32)
         self.part[k, 1] = lax.dot_general(t, self.wu[...], NT, preferred_element_type=F32)
+        self.swap(k, 0, pl.ds(0, 2))
+
+    def swap(self, k, i, arrays):
+        other = pl.ds(pl.multiple_of((1 - self.c) * 64, 64), 64)
+        self.send(("s1", k, i), self.part.at[k, arrays, other, :], self.s1.at[k, arrays], self.dev(c=1 - self.c))
 
     def F(self, k):
         r = self.rows(k)
         self.part[k, 2] = lax.dot_general(self.cot[r, :], self.wd[...], NT, preferred_element_type=F32)
-        other = pl.ds(pl.multiple_of((1 - self.c) * 64, 64), 64)
-        self.send(("s1", k), self.part.at[k, :, other, :], self.s1.at[k], self.dev(c=1 - self.c))
+        self.swap(k, 1, pl.ds(2, 1))
 
     def G(self, k):
-        self.wait(("s1", k), self.s1.at[k], self.dev(c=1 - self.c))
+        for i, arrays in ((0, pl.ds(0, 2)), (1, pl.ds(2, 1))):
+            self.wait(("s1", k, i), self.s1.at[k, arrays], self.dev(c=1 - self.c))
         mine = pl.ds(pl.multiple_of(self.c * 64, 64), 64)
         rest = []
         for i in range(3):

time: 105 us -> 104 us (level)
    pallas_call x1, Pallas kernels: 102 us -> 100 us  [shards(): pl.pallas_call(kernel, out_shape=(vmem((SH, d), BF), vmem((f, d), BF), vm...]
where the time goes in v6:
time: 104 us; the launch traced here: 103 us
  Pallas kernels  103 us (99%)
    pallas_call x1, Pallas kernels, shards(): pl.pallas_call(kernel, out_shape=(vmem((SH, d), BF), vmem((f, d), BF), vm...  100 us
    pallas_call x1, Pallas kernels, shards(): pl.pallas_call(hand_over, out_shape=tuple((jax.ShapeDtypeStruct(r.shape,...  2.49 us

profile of v6, /device:TPU:1, one launch (start us, length us, event | category | flops | bytes accessed | tf_op | source)
XLA Modules:
  0.0 103.4 jit_solution(17789367787860856225)
XLA Ops:
  0.6 100.1 %shard_map.84 = (bf16[16,2048]{1,0:T(8,128)(2,1)S(1)}, bf16[448,2048]{1,0:T(8,128)(2,1)S(1)}, bf16[448,2048]{1,0:T(8,128)(2,1)S(1)}, bf16[448,2048]{1,0:T(8,128)(2,1)S(1)}) custom-call(bf16[16,2048]{1,0:T(8,128)(2,1)} %refs_0_.1, bf16[16,2048]{1,0:T(8,128)(2,1)} %refs_1_.1, bf16[448,2048]{1,0:T(8,128)(2,1)} %bitcast.4, bf16[448,2048]{1,0:T(8,128)(2,1)} %bitcast.5, ...), custom_call_target="tpu_custom_call" | custom-call | flops 15032385536 | bytes 11010048 | tf_op jit(solution)/shard_map/pallas_call | solution.py:452
  100.7 2.5 %shard_map.85 = (bf16[16,2048]{1,0:T(8,128)(2,1)}, bf16[448,2048]{1,0:T(8,128)(2,1)}, bf16[448,2048]{1,0:T(8,128)(2,1)}, bf16[448,2048]{1,0:T(8,128)(2,1)}) custom-call(bf16[16,2048]{1,0:T(8,128)(2,1)S(1)} %get-tuple-element.12.refs_0_, bf16[448,2048]{1,0:T(8,128)(2,1)S(1)} %get-tuple-element.13.refs_1_, bf16[448,2048]{1,0:T(8,128)(2,1)S(1)} %get-tuple-element.14.refs_2_, ...), custom_call_target="tpu_custom_call" | custom-call | tf_op jit(solution)/shard_map/pallas_call | solution.py:478
